TPU v7x, 256 devices: a whole 4x4x8 slice. The times are simulated.
256 devices in a mesh: dp: 4 (over y), coop: 64 (over x, z, core).
Axes of the slice: x: 4, y: 4, z: 8, core: 2. Of those that a mesh axis runs over, the one named last changes fastest.
Arguments:
- features: bfloat16 [131072, 512], P(('dp', 'coop')), parts along dimension 0, may hold values from -6 to 6
- self_first: bfloat16 [512, 256], replicated, may hold values from -0.25 to 0.25
- neighbour_first: bfloat16 [512, 256], replicated, may hold values from -0.25 to 0.25
- bias_first: float32 [256], replicated, may hold values from -3 to 3
- self_second: bfloat16 [256, 256], replicated, may hold values from -0.375 to 0.375
- neighbour_second: bfloat16 [256, 256], replicated, may hold values from -0.375 to 0.375
- bias_second: float32 [256], replicated, may hold values from -3 to 3
- request_first: int32 [256, 64, 16], P(('dp', 'coop')), parts along dimension 0, may hold values from 0 to 511, as said below
- adjacent_first: int32 [131072, 10], P(('dp', 'coop')), parts along dimension 0, may hold values from -1 to 1023, as said below
- request_second: int32 [256, 64, 16], P(('dp', 'coop')), parts along dimension 0, may hold values from 0 to 511, as said below
- adjacent_second: int32 [131072, 10], P(('dp', 'coop')), parts along dimension 0, may hold values from -1 to 1023, as said below
- request_edges: int32 [256, 64, 16], P(('dp', 'coop')), parts along dimension 0, may hold values from 0 to 511, as said below
- edge_source: int32 [131072], P(('dp', 'coop')), parts along dimension 0, may hold values from 0 to 511
- edge_target: int32 [131072], P(('dp', 'coop')), parts along dimension 0, may hold values from 0 to 1023, as said below
Outputs:
- embedding: bfloat16 [131072, 256], P(('dp', 'coop')), parts along dimension 0
- self_first_gradient: float32 [2048, 256], P('dp'), parts along dimension 0
- neighbour_first_gradient: float32 [2048, 256], P('dp'), parts along dimension 0
- bias_first_gradient: float32 [1024], P('dp'), parts along dimension 0
- self_second_gradient: float32 [1024, 256], P('dp'), parts along dimension 0
- neighbour_second_gradient: float32 [1024, 256], P('dp'), parts along dimension 0
- bias_second_gradient: float32 [1024], P('dp'), parts along dimension 0
There are 4 independent parts, one for each index of `dp`. A program takes and returns all parts, laid end to end along the dimension named above; an argument that names none is the same for every part. Nothing has to cross between parts.
Inputs may be any that keep to these rules, and one draw needn't show every extreme that they name: For each device d and owner o the 16 entries request_first[d, o] are distinct rows of o. For each device d and owner o the 16 entries request_second[d, o] are distinct rows of o. For each device d and owner o the 16 entries request_edges[d, o] are distinct rows of o. `adjacent_first`: each row names 1 to 10 slots of its own device, valid entries first and -1 after; some rows have all 10. Slots named by no row of a device are never needed. In every draw some owner has all 16 of its slots named on every device, and every device names its first and its last slot. `adjacent_second`: as adjacent_first, for layer two. `edge_target`: slots of the edge requests of the edge's own device. In every draw some owner has all 16 of its slots named on every device, and every device names its first and its last slot.
All inputs are finite; a program needn't handle non-finite values.
Results may differ from a plain program's by a relative error of at most 0.006.
The roundings to bfloat16 on the way count: a program that leaves them out, or rounds other values in their place, can miss the bound.
Values may be sent and summed in bfloat16 or wider, within the bound.
A program may use at most 64 MiB of HBM per device.

v0:
```python
import jax
import jax.numpy as jnp
from jax import lax
from jax.sharding import PartitionSpec as P


def neighbour_mean(slot_rows, adjacent):
    valid = adjacent >= 0
    safe = jnp.where(valid, adjacent, 0)
    count = jnp.sum(valid.astype(jnp.float32), axis=1)
    total = jnp.zeros((adjacent.shape[0], slot_rows.shape[1]), jnp.float32)
    for column in range(adjacent.shape[1]):
        picked = jnp.take(slot_rows, safe[:, column], axis=0).astype(jnp.float32)
        total = total + jnp.where(valid[:, column : column + 1], picked, 0.0)
    return total / count[:, None]


def slot_totals(grad, adjacent, slots):
    valid = adjacent >= 0
    count = jnp.sum(valid.astype(jnp.float32), axis=1)
    scaled = grad / count[:, None]
    target = jnp.where(valid, adjacent, slots)
    totals = jnp.zeros((slots + 1, grad.shape[1]), jnp.float32)
    for column in range(adjacent.shape[1]):
        totals = totals.at[target[:, column]].add(scaled)
    return totals[:slots]


def per_device(
    features,
    self_first,
    neighbour_first,
    bias_first,
    self_second,
    neighbour_second,
    bias_second,
    request_first,
    adjacent_first,
    request_second,
    adjacent_second,
    request_edges,
    edge_source,
    edge_target,
):
    peers = lax.axis_size("coop")
    width = self_first.shape[1]
    wanted_first = request_first[0]
    wanted_second = request_second[0]
    wanted_edges = request_edges[0]
    slot_count = wanted_first.shape[0] * wanted_first.shape[1]
    edge_slots = wanted_edges.shape[0] * wanted_edges.shape[1]
    asked_first = lax.all_to_all(wanted_first, "coop", split_axis=0, concat_axis=0, tiled=True)
    arrived = lax.all_to_all(
        jnp.take(features, asked_first, axis=0), "coop", split_axis=0, concat_axis=0, tiled=True
    )
    arrived = arrived.reshape(slot_count, features.shape[1])
    projected = jnp.dot(arrived, neighbour_first, preferred_element_type=jnp.float32).astype(
        jnp.bfloat16
    )
    before = (
        jnp.dot(features, self_first, preferred_element_type=jnp.float32)
        + neighbour_mean(projected, adjacent_first)
        + bias_first
    )
    hidden = jnp.maximum(before, 0.0).astype(jnp.bfloat16)
    asked_second = lax.all_to_all(wanted_second, "coop", split_axis=0, concat_axis=0, tiled=True)
    fetched = lax.all_to_all(
        jnp.take(hidden, asked_second, axis=0), "coop", split_axis=0, concat_axis=0, tiled=True
    )
    fetched = fetched.reshape(slot_count, width)
    proj_second = jnp.dot(fetched, neighbour_second, preferred_element_type=jnp.float32).astype(
        jnp.bfloat16
    )
    embedding = (
        jnp.dot(hidden, self_second, preferred_element_type=jnp.float32)
        + neighbour_mean(proj_second, adjacent_second)
        + bias_second
    ).astype(jnp.bfloat16)
    asked_edges = lax.all_to_all(wanted_edges, "coop", split_axis=0, concat_axis=0, tiled=True)
    distant = lax.all_to_all(
        jnp.take(embedding, asked_edges, axis=0), "coop", split_axis=0, concat_axis=0, tiled=True
    )
    distant = distant.reshape(edge_slots, width)
    edges_local = edge_source.shape[0]
    total_edges = edges_local * peers
    left = jnp.take(embedding, edge_source, axis=0).astype(jnp.float32)
    right = jnp.take(distant, edge_target, axis=0).astype(jnp.float32)
    score = jnp.sum(left * right, axis=1) * width ** (-0.5)
    label = (jnp.arange(edges_local) < edges_local // 2).astype(jnp.float32)
    coef = (jax.nn.sigmoid(score) - label) * (total_edges * width) ** (-0.5)
    outer_grad = (
        jnp.zeros((features.shape[0], width), jnp.float32)
        .at[edge_source]
        .add(coef[:, None] * right)
    )
    distant_grad = (
        jnp.zeros((edge_slots, width), jnp.float32).at[edge_target].add(coef[:, None] * left)
    )
    returned = lax.all_to_all(
        distant_grad.reshape(peers, -1, width).astype(jnp.bfloat16),
        "coop",
        split_axis=0,
        concat_axis=0,
        tiled=True,
    ).astype(jnp.float32)
    outer_grad = outer_grad.at[asked_edges.reshape(-1)].add(returned.reshape(-1, width))
    outer_round = outer_grad.astype(jnp.bfloat16)
    self_second_grad = jnp.einsum(
        "vh,vg->hg", hidden, outer_round, preferred_element_type=jnp.float32
    )
    bias_second_grad = jnp.sum(outer_grad, axis=0)
    slot_second = slot_totals(outer_grad, adjacent_second, slot_count).astype(jnp.bfloat16)
    neighbour_second_grad = jnp.einsum(
        "sh,sg->hg", fetched, slot_second, preferred_element_type=jnp.float32
    )
    coming_back = lax.all_to_all(
        slot_second.reshape(peers, -1, width), "coop", split_axis=0, concat_axis=0, tiled=True
    )
    back_terms = jnp.einsum(
        "sg,hg->sh",
        coming_back.reshape(-1, width),
        neighbour_second,
        preferred_element_type=jnp.float32,
    )
    back_hidden = jnp.einsum(
        "vg,hg->vh", outer_round, self_second, preferred_element_type=jnp.float32
    )
    back_hidden = back_hidden.at[asked_second.reshape(-1)].add(back_terms)
    inner = jnp.where(before > 0.0, back_hidden, 0.0)
    inner_round = inner.astype(jnp.bfloat16)
    self_first_grad = jnp.einsum(
        "vf,vh->fh", features, inner_round, preferred_element_type=jnp.float32
    )
    bias_first_grad = jnp.sum(inner, axis=0)
    slot_first = slot_totals(inner, adjacent_first, slot_count).astype(jnp.bfloat16)
    neighbour_first_grad = jnp.einsum(
        "sf,sh->fh", arrived, slot_first, preferred_element_type=jnp.float32
    )
    summed = lax.psum(
        (
            self_first_grad,
            neighbour_first_grad,
            bias_first_grad,
            self_second_grad,
            neighbour_second_grad,
            bias_second_grad,
        ),
        "coop",
    )
    return (embedding, summed[0], summed[1], summed[2], summed[3], summed[4], summed[5])


def solution(mesh):
    in_specs = (
        P(("dp", "coop"), None),
        P(),
        P(),
        P(),
        P(),
        P(),
        P(),
        P(("dp", "coop"), None, None),
        P(("dp", "coop"), None),
        P(("dp", "coop"), None, None),
        P(("dp", "coop"), None),
        P(("dp", "coop"), None, None),
        P(("dp", "coop")),
        P(("dp", "coop")),
    )
    out_specs = (
        P(("dp", "coop"), None),
        P("dp", None),
        P("dp", None),
        P("dp"),
        P("dp", None),
        P("dp", None),
        P("dp"),
    )
    return jax.shard_map(
        per_device, mesh=mesh, in_specs=in_specs, out_specs=out_specs, check_vma=False
    )
```

profile of v0, /device:TPU:1, one launch (start us, length us, event | category | flops | bytes accessed | tf_op | source)
XLA Modules:
  0.0 548.0 jit_solution(10530331851335181913)
XLA Ops:
  8.6 13.0 %all-to-all-start = ((s32[64,1,16]{2,1,0:T(1,128)}), s32[64,1,16]{2,1,0:T(1,128)S(1)}, u32[]{:S(2)}, u32[]{:S(2)}) async-start(s32[64,1,16]{2,1,0:T(1,128)} %bitcast.1), calls=%async_computation | async-start | bytes 65536 | tf_op jit(solution)/shard_map/all_to_all | solution.py:52
  30.8 6.9 %all-to-all-start.2 = ((s32[64,1,16]{2,1,0:T(1,128)}), s32[64,1,16]{2,1,0:T(1,128)S(1)}, u32[]{:S(2)}, u32[]{:S(2)}) async-start(s32[64,1,16]{2,1,0:T(1,128)} %bitcast.16), calls=%async_computation.2 | async-start | bytes 65536 | tf_op jit(solution)/shard_map/all_to_all | solution.py:66
  37.8 4.0 gather_fusion
  43.0 3.9 all-to-all-done.2
  46.9 6.6 %all-to-all-start.1 = ((bf16[64,16,512]{2,1,0:T(8,128)(2,1)}), bf16[64,16,512]{2,1,0:T(8,128)(2,1)S(1)}, u32[]{:S(2)}, u32[]{:S(2)}) async-start(bf16[64,16,512]{2,1,0:T(8,128)(2,1)} %broadcast_select_fusion), calls=%async_computation.1 | async-start | bytes 2097152 | tf_op jit(solution)/shard_map/all_to_all | solution.py:53
  54.4 27.6 %all-to-all-done.1 = bf16[64,16,512]{2,1,0:T(8,128)(2,1)S(1)} async-done(((bf16[64,16,512]{2,1,0:T(8,128)(2,1)}), bf16[64,16,512]{2,1,0:T(8,128)(2,1)S(1)}, u32[]{:S(2)}, u32[]{:S(2)}) %all-to-all-start.1) | async-done | bytes 1048608 | tf_op jit(solution)/shard_map/all_to_all | solution.py:53
  82.0 6.5 %all-to-all-start.4 = ((s32[64,1,16]{2,1,0:T(1,128)}), s32[64,1,16]{2,1,0:T(1,128)S(1)}, u32[]{:S(2)}, u32[]{:S(2)}) async-start(s32[64,1,16]{2,1,0:T(1,128)} %bitcast.29), calls=%async_computation.4 | async-start | bytes 65536 | tf_op jit(solution)/shard_map/all_to_all | solution.py:79
  109.9 4.2 maximum_convert_fusion
  114.0 3.9 gather_fusion.12
  119.0 10.8 %all-to-all-start.3 = ((bf16[64,16,256]{2,1,0:T(8,128)(2,1)}), bf16[64,16,256]{2,1,0:T(8,128)(2,1)S(1)}, u32[]{:S(2)}, u32[]{:S(2)}) async-start(bf16[64,16,256]{2,1,0:T(8,128)(2,1)} %broadcast_select_fusion.2), calls=%async_computation.3 | async-start | bytes 1048576 | tf_op jit(solution)/shard_map/all_to_all | solution.py:67
  130.1 17.0 %all-to-all-done.3 = bf16[64,16,256]{2,1,0:T(8,128)(2,1)S(1)} async-done(((bf16[64,16,256]{2,1,0:T(8,128)(2,1)}), bf16[64,16,256]{2,1,0:T(8,128)(2,1)S(1)}, u32[]{:S(2)}, u32[]{:S(2)}) %all-to-all-start.3) | async-done | bytes 524320 | tf_op jit(solution)/shard_map/all_to_all | solution.py:67
  170.0 4.8 fusion.2
  174.9 3.9 gather_fusion.23
  179.8 6.6 %all-to-all-start.5 = ((bf16[64,16,256]{2,1,0:T(8,128)(2,1)}), bf16[64,16,256]{2,1,0:T(8,128)(2,1)S(1)}, u32[]{:S(2)}, u32[]{:S(2)}) async-start(bf16[64,16,256]{2,1,0:T(8,128)(2,1)} %broadcast_select_fusion.1), calls=%async_computation.5 | async-start | bytes 1048576 | tf_op jit(solution)/shard_map/all_to_all | solution.py:80
  188.5 15.1 %all-to-all-done.5 = bf16[64,16,256]{2,1,0:T(8,128)(2,1)S(1)} async-done(((bf16[64,16,256]{2,1,0:T(8,128)(2,1)}), bf16[64,16,256]{2,1,0:T(8,128)(2,1)S(1)}, u32[]{:S(2)}, u32[]{:S(2)}) %all-to-all-start.5) | async-done | bytes 524320 | tf_op jit(solution)/shard_map/all_to_all | solution.py:80
  210.5 6.3 %all-to-all-start.6 = ((bf16[64,16,256]{2,1,0:T(8,128)(2,1)}), bf16[64,16,256]{2,1,0:T(8,128)(2,1)S(1)}, u32[]{:S(2)}, u32[]{:S(2)}) async-start(bf16[64,16,256]{2,1,0:T(8,128)(2,1)} %bitcast.34), calls=%async_computation.6 | async-start | bytes 1048576 | tf_op jit(solution)/shard_map/all_to_all | solution.py:99
  221.8 12.3 %all-to-all-done.6 = bf16[64,16,256]{2,1,0:T(8,128)(2,1)S(1)} async-done(((bf16[64,16,256]{2,1,0:T(8,128)(2,1)}), bf16[64,16,256]{2,1,0:T(8,128)(2,1)S(1)}, u32[]{:S(2)}, u32[]{:S(2)}) %all-to-all-start.6) | async-done | bytes 524320 | tf_op jit(solution)/shard_map/all_to_all | solution.py:99
  234.1 6.5 %scatter_custom_fusion.2 = f32[512,256]{1,0:T(8,128)S(1)} fusion(f32[512,256]{1,0:T(8,128)S(1)} %scatter_custom_fusion, s32[1024]{0:T(1024)S(1)} %bitcast.145, bf16[1024,256]{1,0:T(8,128)(2,1)S(1)} %bitcast.88), kind=kCustom, calls=%fused_computation.59 | custom fusion | flops 524288 | bytes 1048576 | tf_op jit(solution)/shard_map/scatter-add | solution.py:106
  248.2 3.8 scatter_custom_fusion.5
  252.0 3.8 scatter_custom_fusion.6
  255.8 4.2 scatter_custom_fusion.7
  267.7 3.8 scatter_custom_fusion.10
  271.5 4.0 scatter_custom_fusion.11
  275.5 4.4 scatter_custom_fusion.12
  280.8 6.3 %all-to-all-start.7 = ((bf16[64,16,256]{2,1,0:T(8,128)(2,1)}), bf16[64,16,256]{2,1,0:T(8,128)(2,1)S(1)}, u32[]{:S(2)}, u32[]{:S(2)}) async-start(bf16[64,16,256]{2,1,0:T(8,128)(2,1)} %bitcast.47), calls=%async_computation.7 | async-start | bytes 1048576 | tf_op jit(solution)/shard_map/all_to_all | solution.py:116
  291.9 12.6 %all-to-all-done.7 = bf16[64,16,256]{2,1,0:T(8,128)(2,1)S(1)} async-done(((bf16[64,16,256]{2,1,0:T(8,128)(2,1)}), bf16[64,16,256]{2,1,0:T(8,128)(2,1)S(1)}, u32[]{:S(2)}, u32[]{:S(2)}) %all-to-all-start.7) | async-done | bytes 524320 | tf_op jit(solution)/shard_map/all_to_all | solution.py:116
  304.8 6.3 %scatter_fusion = f32[512,256]{1,0:T(8,128)S(1)} fusion(f32[512,256]{1,0:T(8,128)S(1)} %fusion.20, s32[1024]{0:T(1024)S(1)} %bitcast.135, f32[1024,256]{1,0:T(8,128)S(1)} %fusion.37), kind=kCustom, calls=%fused_computation.38 | custom fusion | flops 262144 | bytes 3149824 | tf_op jit(solution)/shard_map/scatter-add | solution.py:128
  316.1 3.9 scatter_fusion.1
  334.8 3.9 scatter_fusion.6
  346.3 4.2 scatter_fusion.9
  353.1 124.2 %all-reduce = (f32[256]{0:T(256)}, f32[256]{0:T(256)}) all-reduce(f32[256]{0:T(256)S(1)} %get-tuple-element.60, f32[256]{0:T(256)S(1)} %reduce_sum.57), channel_id=1, replica_groups=mesh['dp'=4,'coop'=64] {'coop'}, use_global_device_ids=true, to_apply=%region_30.33 | all-reduce | flops 512 | bytes 4096 | tf_op jit(solution)/shard_map/psum | solution.py:139
  477.3 59.1 %all-reduce.4.cloned.1.call-done = (f32[512,256]{0,1:T(8,128)}, f32[512,256]{1,0:T(8,128)}, f32[256,256]{1,0:T(8,128)}, f32[256,256]{1,0:T(8,128)}) async-done(((f32[512,256]{0,1:T(8,128)}, f32[512,256]{1,0:T(8,128)}, f32[256,256]{1,0:T(8,128)}, f32[256,256]{1,0:T(8,128)}), (f32[512,256]{0,1:T(8,128)}, f32[512,256]{1,0:T(8,128)}, f32[256,256]{1,0:T(8,128)}, ...) | async-done | bytes 1572880 | tf_op jit(solution)/shard_map/psum | solution.py:139
  (203 shorter events, 127.8 us)
Async XLA Ops:
  7.2 30.7 %copy-start = (bf16[512,512]{1,0:T(8,128)(2,1)S(1)}, bf16[512,512]{1,0:T(8,128)(2,1)}, u32[]{:S(2)}) copy-start(bf16[512,512]{1,0:T(8,128)(2,1)} %param.18) | copy-start | bytes 1572868
  8.6 22.2 %all-to-all-start = ((s32[64,1,16]{2,1,0:T(1,128)}), s32[64,1,16]{2,1,0:T(1,128)S(1)}, u32[]{:S(2)}, u32[]{:S(2)}) async-start(s32[64,1,16]{2,1,0:T(1,128)} %bitcast.1), calls=%async_computation | async-start | bytes 65536 | tf_op jit(solution)/shard_map/all_to_all | solution.py:52
  30.8 16.1 %all-to-all-start.2 = ((s32[64,1,16]{2,1,0:T(1,128)}), s32[64,1,16]{2,1,0:T(1,128)S(1)}, u32[]{:S(2)}, u32[]{:S(2)}) async-start(s32[64,1,16]{2,1,0:T(1,128)} %bitcast.16), calls=%async_computation.2 | async-start | bytes 65536 | tf_op jit(solution)/shard_map/all_to_all | solution.py:66
  43.0 10.5 %copy-start.22 = (s32[1,64,16]{1,2,0:T(8,128)S(1)}, s32[1,64,16]{1,2,0:T(8,128)}, u32[]{:S(2)}) copy-start(s32[1,64,16]{1,2,0:T(8,128)} %param.29) | copy-start | bytes 12292
  43.0 45.6 %copy-start.8 = (bf16[512,256]{1,0:T(8,128)(2,1)S(1)}, bf16[512,256]{1,0:T(8,128)(2,1)}, u32[]{:S(2)}) copy-start(bf16[512,256]{1,0:T(8,128)(2,1)} %param.20) | copy-start | bytes 786436
  46.9 35.1 %all-to-all-start.1 = ((bf16[64,16,512]{2,1,0:T(8,128)(2,1)}), bf16[64,16,512]{2,1,0:T(8,128)(2,1)S(1)}, u32[]{:S(2)}, u32[]{:S(2)}) async-start(bf16[64,16,512]{2,1,0:T(8,128)(2,1)} %broadcast_select_fusion), calls=%async_computation.1 | async-start | bytes 2097152 | tf_op jit(solution)/shard_map/all_to_all | solution.py:53
  82.0 8.9 %copy-start.2 = (bf16[64,16,512]{2,1,0:T(8,128)(2,1)}, bf16[64,16,512]{2,1,0:T(8,128)(2,1)S(1)}, u32[]{:S(2)}) copy-start(bf16[64,16,512]{2,1,0:T(8,128)(2,1)S(1)} %all-to-all-done.1) | copy-start | bytes 3145732
  82.0 37.0 %all-to-all-start.4 = ((s32[64,1,16]{2,1,0:T(1,128)}), s32[64,1,16]{2,1,0:T(1,128)S(1)}, u32[]{:S(2)}, u32[]{:S(2)}) async-start(s32[64,1,16]{2,1,0:T(1,128)} %bitcast.29), calls=%async_computation.4 | async-start | bytes 65536 | tf_op jit(solution)/shard_map/all_to_all | solution.py:79
  107.3 2.6 copy-start.25
  118.0 29.1 %copy-start.7 = (bf16[256,256]{1,0:T(8,128)(2,1)S(1)}, bf16[256,256]{1,0:T(8,128)(2,1)}, u32[]{:S(2)}) copy-start(bf16[256,256]{1,0:T(8,128)(2,1)} %param.23) | copy-start | bytes 393220
  119.0 28.0 %all-to-all-start.3 = ((bf16[64,16,256]{2,1,0:T(8,128)(2,1)}), bf16[64,16,256]{2,1,0:T(8,128)(2,1)S(1)}, u32[]{:S(2)}, u32[]{:S(2)}) async-start(bf16[64,16,256]{2,1,0:T(8,128)(2,1)} %broadcast_select_fusion.2), calls=%async_computation.3 | async-start | bytes 1048576 | tf_op jit(solution)/shard_map/all_to_all | solution.py:67
  167.5 2.6 copy-start.26
  174.9 11.7 %copy-start.1 = (bf16[512,256]{1,0:T(8,128)(2,1)}, bf16[512,256]{1,0:T(8,128)(2,1)S(1)}, u32[]{:S(2)}) copy-start(bf16[512,256]{1,0:T(8,128)(2,1)S(1)} %fusion.2) | copy-start | bytes 786436
  178.8 7.6 %copy-start.24 = (s32[512]{0:T(512)S(1)}, s32[512]{0:T(512)}, u32[]{:S(2)}) copy-start(s32[512]{0:T(512)} %param.31) | copy-start | bytes 6148
  178.8 7.6 %copy-start.23 = (s32[512]{0:T(512)S(1)}, s32[512]{0:T(512)}, u32[]{:S(2)}) copy-start(s32[512]{0:T(512)} %param.30) | copy-start | bytes 6148
  179.8 23.8 %all-to-all-start.5 = ((bf16[64,16,256]{2,1,0:T(8,128)(2,1)}), bf16[64,16,256]{2,1,0:T(8,128)(2,1)S(1)}, u32[]{:S(2)}, u32[]{:S(2)}) async-start(bf16[64,16,256]{2,1,0:T(8,128)(2,1)} %broadcast_select_fusion.1), calls=%async_computation.5 | async-start | bytes 1048576 | tf_op jit(solution)/shard_map/all_to_all | solution.py:80
  210.5 23.6 %all-to-all-start.6 = ((bf16[64,16,256]{2,1,0:T(8,128)(2,1)}), bf16[64,16,256]{2,1,0:T(8,128)(2,1)S(1)}, u32[]{:S(2)}, u32[]{:S(2)}) async-start(bf16[64,16,256]{2,1,0:T(8,128)(2,1)} %bitcast.34), calls=%async_computation.6 | async-start | bytes 1048576 | tf_op jit(solution)/shard_map/all_to_all | solution.py:99
  279.9 7.2 %copy-start.12 = (s32[512,10]{0,1:T(8,128)S(1)}, s32[512,10]{0,1:T(8,128)}, u32[]{:S(2)}) copy-start(s32[512,10]{0,1:T(8,128)} %get-tuple-element.56) | copy-start | bytes 61444
  280.8 23.7 %all-to-all-start.7 = ((bf16[64,16,256]{2,1,0:T(8,128)(2,1)}), bf16[64,16,256]{2,1,0:T(8,128)(2,1)S(1)}, u32[]{:S(2)}, u32[]{:S(2)}) async-start(bf16[64,16,256]{2,1,0:T(8,128)(2,1)} %bitcast.47), calls=%async_computation.7 | async-start | bytes 1048576 | tf_op jit(solution)/shard_map/all_to_all | solution.py:116
  287.1 249.3 %all-reduce.4.cloned.1.call-start = ((), (), s32[]{:S(2)}) async-start(), calls=%async_computation.8 | async-start | bytes 3145728 | tf_op jit(solution)/shard_map/psum | solution.py:139
  304.8 6.3 %copy-start.5 = (f32[512,256]{1,0:T(8,128)S(1)}, f32[512,256]{1,0:T(8,128)}, u32[]{:S(2)}) copy-start(f32[512,256]{1,0:T(8,128)} %get-tuple-element.103) | copy-start | bytes 1572868
  312.4 3.7 copy-start.21
  316.1 3.9 copy-start.20
  320.0 3.7 copy-start.19
  323.7 3.7 copy-start.18
  327.4 3.7 copy-start.17
  331.1 3.7 copy-start.16
  334.8 3.9 copy-start.15
  338.7 3.7 copy-start.14
  342.5 3.8 copy-start.13
  536.4 2.9 copy-start.10
  536.4 3.6 copy-start.9
  (4 other events, 9.1 us)
Sparse Core Ops, SparseCore 0:
  353.1 183.2 all-reduce.3
where the time goes:
time: 555 us; the launch traced here: 548 us
  waiting for transfers between devices  151 us (27%)
  blocking collectives  124 us (22%)
  other arithmetic  108 us (19%)
  local copies, waits for them, and re-layouts  69.1 us (12%)
  starting transfers between devices  63 us (11%)
  matrix products  16.9 us (3%)
  between operations  15.7 us (3%)
    psum x1, blocking collectives, per_device(): lax.psum((self_first_grad, neighbour_first_grad, bias_first_grad, self_se...  124 us
    scatter-add x20, other arithmetic, slot_totals(): totals = totals.at[target[:, column]].add(scaled)  77 us
    psum x1, waiting for transfers between devices, per_device(): lax.psum((self_first_grad, neighbour_first_grad, bias_first_grad, self_se...  59.1 us
    gather x20, local copies, waits for them, and re-layouts, neighbour_mean(): picked = jnp.take(slot_rows, safe[:, column], axis=0).astype(jnp.float32)  43.4 us
    all_to_all x1, waiting for transfers between devices, per_device(): lax.all_to_all(jnp.take(features, asked_first, axis=0), 'coop', split_axi...  27.6 us
    all_to_all x1, waiting for transfers between devices, per_device(): lax.all_to_all(jnp.take(hidden, asked_second, axis=0), 'coop', split_axis...  17 us
    all_to_all x1, waiting for transfers between devices, per_device(): lax.all_to_all(jnp.take(embedding, asked_edges, axis=0), 'coop', split_ax...  15.1 us
    all_to_all x1, starting transfers between devices, per_device(): lax.all_to_all(wanted_first, 'coop', split_axis=0, concat_axis=0, tiled=T...  13 us
  transfers between devices with their start and end apart: 9, of which 8 were waited for; matrix products, arithmetic and copies ran while one was open for 10% of the time, Pallas kernels for 0%

commit v1 on v0

v1 whole, which is shorter than its diff:
```python
import functools

import jax
import jax.numpy as jnp
from jax import lax
from jax.experimental import pallas as pl
from jax.experimental.pallas import tpu as pltpu
from jax.sharding import PartitionSpec as P

MESH = pl.DeviceIdType.MESH
BF = jnp.bfloat16
F32 = jnp.float32
CHUNK = 256


def nn(a, b):
    return lax.dot_general(a, b, (((1,), (0,)), ((), ())), preferred_element_type=F32)


def nt(a, b):
    return lax.dot_general(a, b, (((1,), (1,)), ((), ())), preferred_element_type=F32)


def split(value):
    high = value.astype(BF)
    low = (value - high.astype(F32)).astype(BF)
    return high, low


def blocks(total, step, body):
    def one(i, carry):
        body(pl.ds(pl.multiple_of(i * step, step), step), i * step)
        return carry

    lax.fori_loop(0, total // step, one, 0)


def one_if(flag):
    return jnp.where(flag, 1.0, 0.0).astype(BF)


def kernel(
    peers,
    features,
    self_first,
    neighbour_first,
    bias_first,
    self_second,
    neighbour_second,
    bias_second,
    request_first,
    adjacent_first,
    request_second,
    adjacent_second,
    request_edges,
    edge_source,
    edge_target,
    embedding,
    out_self_first,
    out_neighbour_first,
    out_bias_first,
    out_self_second,
    out_neighbour_second,
    out_bias_second,
    ask_send,
    ask_recv,
    asked,
    a1,
    a1t,
    a2,
    a2t,
    p1,
    p1t,
    p2,
    p2t,
    p3,
    p3t,
    source_t,
    source,
    target_t,
    target,
    features_t,
    hidden_t,
    inv1,
    inv2,
    base,
    before,
    hidden,
    left,
    grad,
    own,
    totals,
    sends,
    recvs,
    bias_send,
    bias_recv,
    gradients,
    pair_recv,
    shard_send,
    shard_recv,
    final,
    send_sems,
    recv_sems,
):
    me = lax.axis_index("coop")
    chip = me // 2
    core = me % 2
    chips = peers // 2
    nodes, width = hidden.shape
    feats = features.shape[1]
    slots = a1.shape[1]
    edges = edge_source.shape[1]
    cap = slots // peers

    barrier = pltpu.get_barrier_semaphore()

    def greet(k, carry):
        pl.semaphore_signal(
            barrier, inc=1, device_id={"coop": (me + k) % peers}, device_id_type=MESH
        )
        return carry

    lax.fori_loop(1, peers, greet, 0)

    for d in range(peers):
        for n, request in enumerate((request_first, request_second, request_edges)):
            ask_send[d, :, cap * n : cap * (n + 1)] = request[d : d + 1, :]

    def counts(adjacent, matrix, inverse):
        step = 32

        def fill(rows, start):
            table = adjacent[rows, :]
            inverse[rows, :] = 1.0 / jnp.sum((table >= 0).astype(F32), axis=1, keepdims=True)
            lanes = lax.broadcasted_iota(jnp.int32, (step, slots), 1)
            total = jnp.zeros((step, slots), F32)
            for j in range(table.shape[1]):
                total = total + jnp.where(table[:, j : j + 1] == lanes, 1.0, 0.0)
            matrix[rows, :] = total.astype(BF)

        blocks(nodes, step, fill)

    def transpose(src, dst):
        def one(rows, start):
            dst[rows, :] = src[:, rows].T

        blocks(src.shape[1], 128, one)

    counts(adjacent_first, a1, inv1)
    counts(adjacent_second, a2, inv2)

    def node_base(rows, start):
        totals[rows, :] = nn(features[rows, :], neighbour_first[...])
        base[rows, :] = nn(features[rows, :], self_first[...]) + bias_first[...]

    blocks(nodes, CHUNK, node_base)
    projected = totals[...].astype(BF)
    hidden[...] = projected

    pl.semaphore_wait(barrier, peers - 1)

    def ask(k, carry):
        peer = (me + k) % peers
        pltpu.make_async_remote_copy(
            ask_send.at[peer],
            ask_recv.at[me],
            send_sems.at[0],
            recv_sems.at[0],
            device_id={"coop": peer},
            device_id_type=MESH,
        ).start()
        return carry

    lax.fori_loop(1, peers, ask, 0)
    ask_recv[pl.ds(me, 1)] = ask_send[pl.ds(me, 1)]
    others = pl.ds(0, peers - 1)
    pltpu.make_async_copy(ask_recv.at[others], ask_recv.at[others], recv_sems.at[0]).wait()
    for d in range(peers):
        asked[d : d + 1, :] = ask_recv[d]

    def picks(n, rows_matrix, columns_matrix):
        table = asked[...]
        high = table - (table % 16)
        parts = jnp.concatenate([high, table % 16], axis=1).astype(F32).astype(BF)
        step = min(CHUNK, slots)

        def one(rows, start):
            row = lax.broadcasted_iota(jnp.int32, (step, peers), 0) + start
            owner = lax.broadcasted_iota(jnp.int32, (step, peers), 1)
            spread = nn(one_if(row // cap == owner), parts)
            row = lax.broadcasted_iota(jnp.int32, spread.shape, 0) + start
            lane = lax.broadcasted_iota(jnp.int32, spread.shape, 1) % 128
            mine = jnp.where(lane == n * cap + row % cap, spread, 0.0).astype(BF)
            ones = jnp.ones((nodes, spread.shape[1]), BF)
            wanted = nt(mine, ones)
            rows_matrix[rows, :] = one_if(
                wanted == lax.broadcasted_iota(jnp.int32, wanted.shape, 1).astype(F32)
            )
            wanted_t = nt(ones, mine)
            columns_matrix[:, rows] = one_if(
                wanted_t == lax.broadcasted_iota(jnp.int32, wanted_t.shape, 0).astype(F32)
            )

        blocks(slots, step, one)

    def exchange(phase):
        def send(k, carry):
            peer = (me + k) % peers
            pltpu.make_async_remote_copy(
                sends.at[phase, pl.ds(pl.multiple_of(peer * cap, cap), cap)],
                recvs.at[phase, pl.ds(pl.multiple_of(me * cap, cap), cap)],
                send_sems.at[1 + phase],
                recv_sems.at[1 + phase],
                device_id={"coop": peer},
                device_id_type=MESH,
            ).start()
            return carry

        lax.fori_loop(1, peers, send, 0)
        mine = pl.ds(pl.multiple_of(me * cap, cap), cap)
        recvs[phase, mine, :] = sends[phase, mine, :]

    def arrived(phase):
        most = recvs.at[phase, pl.ds(0, (peers - 1) * cap)]
        pltpu.make_async_copy(most, most, recv_sems.at[1 + phase]).wait()

    def fill_rows(phase, matrix, rows_of):
        def one(rows, start):
            sends[phase, rows, :] = nn(matrix[rows, :], rows_of[...]).astype(BF)

        blocks(slots, min(CHUNK, slots), one)

    def fill_split(phase, matrix, value):
        high, low = split(value)

        def one(rows, start):
            part = matrix[rows, :]
            sends[phase, rows, :] = (nn(part, high) + nn(part, low)).astype(BF)

        blocks(slots, min(CHUNK, slots), one)

    picks(0, p1, p1t)
    fill_rows(0, p1, hidden)
    exchange(0)
    picks(1, p2, p2t)
    picks(2, p3, p3t)
    transpose(a1, a1t)
    transpose(a2, a2t)
    transpose(features, features_t)
    vertex = lax.broadcasted_iota(jnp.int32, (nodes, edges), 0)
    source_t[...] = one_if(vertex == edge_source[...])
    slot = lax.broadcasted_iota(jnp.int32, (slots, edges), 0)
    target_t[...] = one_if(slot == edge_target[...])
    transpose(source_t, source)
    transpose(target_t, target)
    arrived(0)

    def layer_one(rows, start):
        value = base[rows, :] + nn(a1[rows, :], recvs[0]) * inv1[rows, :]
        before[rows, :] = value
        hidden[rows, :] = jnp.maximum(value, 0.0).astype(BF)

    blocks(nodes, CHUNK, layer_one)

    def project(rows, start):
        left[rows, :] = nn(hidden[rows, :], neighbour_second[...]).astype(BF)

    blocks(nodes, CHUNK, project)
    fill_rows(1, p2, left)
    exchange(1)

    def second_base(rows, start):
        base[rows, :] = nn(hidden[rows, :], self_second[...]) + bias_second[...]

    blocks(nodes, CHUNK, second_base)
    transpose(hidden, hidden_t)
    arrived(1)

    def layer_two(rows, start):
        embedding[rows, :] = (
            base[rows, :] + nn(a2[rows, :], recvs[1]) * inv2[rows, :]
        ).astype(BF)

    blocks(nodes, CHUNK, layer_two)

    fill_rows(2, p3, embedding)
    exchange(2)

    def lefts(rows, start):
        left[rows, :] = nn(source[rows, :], embedding[...]).astype(BF)

    blocks(edges, CHUNK, lefts)
    arrived(2)

    def scores(rows, start):
        right = nn(target[rows, :], recvs[2])
        here = left[rows, :].astype(F32)
        score = jnp.sum(here * right, axis=1, keepdims=True) * width ** (-0.5)
        edge = lax.broadcasted_iota(jnp.int32, score.shape, 0) + start
        label = jnp.where(edge < edges // 2, 1.0, 0.0)
        coef = (jax.nn.sigmoid(score) - label) * (edges * peers * width) ** (-0.5)
        grad[rows, :] = coef * here
        own[rows, :] = coef * right

    blocks(edges, CHUNK, scores)
    fill_split(3, target_t, grad[...])
    exchange(3)
    high, low = split(own[...])
    totals[...] = nn(source_t[...], high) + nn(source_t[...], low)
    arrived(3)

    def outer(rows, start):
        grad[rows, :] = totals[rows, :] + nn(p3t[rows, :], recvs[3])

    blocks(nodes, CHUNK, outer)
    outer_round = grad[...].astype(BF)
    fill_split(4, a2t, grad[...] * inv2[...])
    exchange(4)
    bias_send[:, :, :width] = jnp.sum(grad[...], axis=0, keepdims=True)[None]
    self_rows = 2 * feats
    near_rows = 2 * feats + width
    gradients[self_rows : self_rows + width, :] = nn(hidden_t[...], outer_round)
    own[...] = nt(outer_round, self_second[...])
    arrived(4)

    def second_totals(rows, start):
        totals[rows, :] = nn(p2t[rows, :], recvs[4])

    blocks(nodes, CHUNK, second_totals)
    high, low = split(totals[...])
    value = own[...] + nt(high, neighbour_second[...]) + nt(low, neighbour_second[...])
    inner = jnp.where(before[...] > 0.0, value, 0.0)
    grad[...] = inner
    fill_split(5, a1t, inner * inv1[...])
    exchange(5)
    gradients[near_rows : near_rows + width, :] = nn(hidden_t[...], high) + nn(hidden_t[...], low)
    bias_send[:, :, width:] = jnp.sum(grad[...], axis=0, keepdims=True)[None]

    def bias(k, carry):
        peer = (me + k) % peers
        pltpu.make_async_remote_copy(
            bias_send.at[0],
            bias_recv.at[me],
            send_sems.at[7],
            recv_sems.at[7],
            device_id={"coop": peer},
            device_id_type=MESH,
        ).start()
        return carry

    lax.fori_loop(1, peers, bias, 0)
    bias_recv[pl.ds(me, 1)] = bias_send[...]
    inner_round = grad[...].astype(BF)

    def self_gradient(rows, start):
        gradients[rows, :] = nn(features_t[rows, :], inner_round)

    blocks(feats, CHUNK, self_gradient)
    pltpu.make_async_copy(bias_recv.at[others], bias_recv.at[others], recv_sems.at[7]).wait()
    total = bias_recv[0]
    for d in range(1, peers):
        total = total + bias_recv[d]
    out_bias_second[...] = total[:, :width]
    out_bias_first[...] = total[:, width:]
    arrived(5)

    def first_totals(rows, start):
        totals[rows, :] = nn(p1t[rows, :], recvs[5])

    blocks(nodes, CHUNK, first_totals)
    high, low = split(totals[...])

    def near_gradient(rows, start):
        part = features_t[rows, :]
        gradients[pl.ds(pl.multiple_of(start + feats, CHUNK), CHUNK), :] = nn(part, high) + nn(
            part, low
        )

    blocks(feats, CHUNK, near_gradient)

    half = gradients.shape[0] // 2
    share = half // chips
    kept = pl.ds(pl.multiple_of(core * half, 8), half)
    given = pl.ds(pl.multiple_of((1 - core) * half, 8), half)
    partner = chip * 2 + 1 - core
    pair = pltpu.make_async_remote_copy(
        gradients.at[given],
        pair_recv,
        send_sems.at[8],
        recv_sems.at[8],
        device_id={"coop": partner},
        device_id_type=MESH,
    )
    pair.start()
    pair.wait_recv()
    shard_send[...] = gradients[kept, :] + pair_recv[...]

    def scatter(k, carry):
        to = (chip + k) % chips
        pltpu.make_async_remote_copy(
            shard_send.at[pl.ds(pl.multiple_of(to * share, 8), share)],
            shard_recv.at[pl.ds(pl.multiple_of(chip * share, 8), share)],
            send_sems.at[9],
            recv_sems.at[9],
            device_id={"coop": to * 2 + core},
            device_id_type=MESH,
        ).start()
        return carry

    lax.fori_loop(1, chips, scatter, 0)
    here = pl.ds(pl.multiple_of(chip * share, 8), share)
    shard_recv[here, :] = shard_send[here, :]
    most = shard_recv.at[pl.ds(0, (chips - 1) * share)]
    pltpu.make_async_copy(most, most, recv_sems.at[9]).wait()
    total = shard_recv[0:share, :]
    for c in range(1, chips):
        total = total + shard_recv[c * share : (c + 1) * share, :]
    place = pl.ds(pl.multiple_of(core * half + chip * share, 8), share)
    final[place, :] = total

    def gather(k, carry):
        to = (chip + k) % chips
        pltpu.make_async_remote_copy(
            final.at[place],
            final.at[place],
            send_sems.at[10],
            recv_sems.at[10],
            device_id={"coop": to * 2 + core},
            device_id_type=MESH,
        ).start()
        return carry

    lax.fori_loop(1, chips, gather, 0)
    pltpu.make_async_copy(most, most, recv_sems.at[10]).wait()
    back = pltpu.make_async_remote_copy(
        final.at[kept],
        final.at[kept],
        send_sems.at[11],
        recv_sems.at[11],
        device_id={"coop": partner},
        device_id_type=MESH,
    )
    back.start()
    back.wait_recv()
    out_self_first[...] = final[:feats, :]
    out_neighbour_first[...] = final[feats : 2 * feats, :]
    out_self_second[...] = final[self_rows : self_rows + width, :]
    out_neighbour_second[...] = final[near_rows : near_rows + width, :]

    pltpu.make_async_copy(ask_send.at[others], ask_send.at[others], send_sems.at[0]).wait()
    for phase in range(6):
        sent = sends.at[phase, pl.ds(0, (peers - 1) * cap)]
        pltpu.make_async_copy(sent, sent, send_sems.at[1 + phase]).wait()
    pltpu.make_async_copy(bias_recv.at[others], bias_recv.at[others], send_sems.at[7]).wait()
    pair.wait_send()
    pltpu.make_async_copy(most, most, send_sems.at[9]).wait()
    pltpu.make_async_copy(most, most, send_sems.at[10]).wait()
    back.wait_send()


def per_device(
    features,
    self_first,
    neighbour_first,
    bias_first,
    self_second,
    neighbour_second,
    bias_second,
    request_first,
    adjacent_first,
    request_second,
    adjacent_second,
    request_edges,
    edge_source,
    edge_target,
):
    nodes, feats = features.shape
    width = self_first.shape[1]
    _, peers, cap = request_first.shape
    slots = peers * cap
    edges = edge_source.shape[0]
    rows = 2 * feats + 2 * width
    vmem = pltpu.VMEM
    scratch = [
        vmem((peers, 1, 128), jnp.int32),
        vmem((peers, 1, 128), jnp.int32),
        vmem((peers, 128), jnp.int32),
        vmem((nodes, slots), BF),
        vmem((slots, nodes), BF),
        vmem((nodes, slots), BF),
        vmem((slots, nodes), BF),
        vmem((slots, nodes), BF),
        vmem((nodes, slots), BF),
        vmem((slots, nodes), BF),
        vmem((nodes, slots), BF),
        vmem((slots, nodes), BF),
        vmem((nodes, slots), BF),
        vmem((nodes, edges), BF),
        vmem((edges, nodes), BF),
        vmem((slots, edges), BF),
        vmem((edges, slots), BF),
        vmem((feats, nodes), BF),
        vmem((width, nodes), BF),
        vmem((nodes, 1), F32),
        vmem((nodes, 1), F32),
        vmem((nodes, width), F32),
        vmem((nodes, width), F32),
        vmem((nodes, width), BF),
        vmem((nodes, width), BF),
        vmem((nodes, width), F32),
        vmem((nodes, width), F32),
        vmem((nodes, width), F32),
        vmem((6, slots, width), BF),
        vmem((6, slots, width), BF),
        vmem((1, 1, 2 * width), F32),
        vmem((peers, 1, 2 * width), F32),
        vmem((rows, width), F32),
        vmem((rows // 2, width), F32),
        vmem((rows // 2, width), F32),
        vmem((rows // 2, width), F32),
        vmem((rows, width), F32),
        pltpu.SemaphoreType.DMA((12,)),
        pltpu.SemaphoreType.DMA((12,)),
    ]
    results = pl.pallas_call(
        functools.partial(kernel, peers),
        out_shape=(
            jax.ShapeDtypeStruct((nodes, width), BF),
            jax.ShapeDtypeStruct((feats, width), F32),
            jax.ShapeDtypeStruct((feats, width), F32),
            jax.ShapeDtypeStruct((1, width), F32),
            jax.ShapeDtypeStruct((width, width), F32),
            jax.ShapeDtypeStruct((width, width), F32),
            jax.ShapeDtypeStruct((1, width), F32),
        ),
        in_specs=[pl.BlockSpec(memory_space=vmem)] * 14,
        out_specs=[pl.BlockSpec(memory_space=vmem)] * 7,
        scratch_shapes=scratch,
        compiler_params=pltpu.CompilerParams(
            collective_id=0, has_side_effects=True, vmem_limit_bytes=52 * 2**20
        ),
    )(
        features,
        self_first,
        neighbour_first,
        bias_first.reshape(1, width),
        self_second,
        neighbour_second,
        bias_second.reshape(1, width),
        request_first[0],
        adjacent_first,
        request_second[0],
        adjacent_second,
        request_edges[0],
        edge_source.reshape(1, edges),
        edge_target.reshape(1, edges),
    )
    return (
        results[0],
        results[1],
        results[2],
        results[3].reshape(width),
        results[4],
        results[5],
        results[6].reshape(width),
    )


def solution(mesh):
    in_specs = (
        P(("dp", "coop"), None),
        P(),
        P(),
        P(),
        P(),
        P(),
        P(),
        P(("dp", "coop"), None, None),
        P(("dp", "coop"), None),
        P(("dp", "coop"), None, None),
        P(("dp", "coop"), None),
        P(("dp", "coop"), None, None),
        P(("dp", "coop")),
        P(("dp", "coop")),
    )
    out_specs = (
        P(("dp", "coop"), None),
        P("dp", None),
        P("dp", None),
        P("dp"),
        P("dp", None),
        P("dp", None),
        P("dp"),
    )
    return jax.shard_map(
        per_device, mesh=mesh, in_specs=in_specs, out_specs=out_specs, check_vma=False
    )
```

time: 555 us -> 187 us (0.34); the launches traced: 548 us -> 187 us
  Pallas kernels: 0 us -> 176 us
  waiting for transfers between devices: 151 us -> 0 us
  blocking collectives: 124 us -> 0 us
  other arithmetic: 108 us -> 0 us
  starting transfers between devices: 63 us -> 0 us
  local copies, waits for them, and re-layouts: 69.1 us -> 9.94 us
  matrix products: 16.9 us -> 0 us
  between operations: 15.7 us -> 0.79 us
    pallas_call x0 -> x1, Pallas kernels: none -> 176 us  [per_device(): pl.pallas_call(functools.partial(kernel, peers), out_shape=(jax.ShapeDtyp...]
    psum x1 -> x0, blocking collectives: 124 us -> none  [per_device(): lax.psum((self_first_grad, neighbour_first_grad, bias_first_grad, self_se...]
    scatter-add x24 -> x0, other arithmetic: 97.3 us -> none  [the longest x20 77 us: slot_totals(): totals = totals.at[target[:, column]].add(scaled)]
    all_to_all x8 -> x0, waiting for transfers between devices: 92 us -> none  [the longest x1 27.6 us: per_device(): lax.all_to_all(jnp.take(features, asked_first, axis=0), 'coop', split_axi...]
    all_to_all x8 -> x0, starting transfers between devices: 62.9 us -> none  [the longest x1 13 us: per_device(): lax.all_to_all(wanted_first, 'coop', split_axis=0, concat_axis=0, tiled=T...]
    gather x25 -> x0, local copies, waits for them, and re-layouts: 59.2 us -> none  [the longest x20 43.4 us: neighbour_mean(): picked = jnp.take(slot_rows, safe[:, column], axis=0).astype(jnp.float32)]
    psum x1 -> x0, waiting for transfers between devices: 59.1 us -> none  [per_device(): lax.psum((self_first_grad, neighbour_first_grad, bias_first_grad, self_se...]
    dot_general x10 -> x0, matrix products: 16.9 us -> none  [the longest x1 4.81 us: per_device(): jnp.dot(hidden, self_second, preferred_element_type=jnp.float32)]
  transfers between devices with their start and end apart: 9 -> 0, of which waited for: 8 -> 0; matrix products, arithmetic and copies ran while one was open for 10% -> 0% of each run, Pallas kernels for 0% -> 0%
where the time goes in v1:
time: 187 us
  Pallas kernels  176 us (94%)
  local copies, waits for them, and re-layouts  9.94 us (5%)
    pallas_call x1, Pallas kernels, per_device(): pl.pallas_call(functools.partial(kernel, peers), out_shape=(jax.ShapeDtyp...  176 us
    unnamed x38, local copies, waits for them, and re-layouts  9.94 us

profile of v1, /device:TPU:1, one launch (start us, length us, event | category | flops | bytes accessed | tf_op | source)
XLA Modules:
  0.0 187.1 jit_solution(14219488618355156099)
XLA Ops:
  0.6 0.0 copy-start.11
  0.6 0.0 copy-start.10
  0.7 0.8 copy.21
  1.5 0.0 copy-start.2
  1.5 0.1 copy.22
  1.6 0.6 copy-done.12
  2.1 0.1 copy.23
  2.2 0.0 copy-start.1
  2.2 0.1 copy.24.adjacent_first
  2.4 0.0 copy-start.4
  2.4 0.0 copy-start.5
  2.4 0.0 copy-start.6
  2.4 0.0 copy-start.7
  2.4 1.6 copy.25.adjacent_second
  4.1 0.0 copy-done.1
  4.1 0.0 copy-done.4
  4.1 0.0 copy-done.5
  4.1 0.0 copy-done.6
  4.1 0.0 copy-done.7
  4.1 0.0 copy-start.3
  4.1 0.9 copy-done.3
  5.0 176.4 %shard_map.189 = (bf16[512,256]{1,0:T(8,128)(2,1)S(1)}, f32[512,256]{1,0:T(8,128)}, f32[512,256]{1,0:T(8,128)}, f32[1,256]{1,0:T(1,128)S(1)}, f32[256,256]{1,0:T...) custom-call(bf16[512,512]{1,0:T(8,128)(2,1)} %features.1, bf16[512,256]{1,0:T(8,128)(2,1)S(1)} %copy-done, ...), custom_call_target="tpu_custom_call" | custom-call | tf_op jit(solution)/shard_map/pallas_call | solution.py:525
  181.4 0.0 copy-start.9
  181.4 0.7 copy.33
  182.1 0.4 copy-done.9
  182.6 0.8 copy.34
  183.4 0.4 copy-done.8
  183.8 0.8 copy.35
  184.6 0.6 copy.36
  185.2 0.7 copy.37
  185.9 0.7 copy.38
  186.6 0.6 copy.39
  (7 shorter events, 0.0 us)
Async XLA Ops:
  0.6 0.8 copy-start.11
  0.6 1.6 copy-start.10
  1.4 0.7 copy-start.12
  1.5 2.6 %copy-start.2 = (bf16[256,256]{1,0:T(8,128)(2,1)S(1)}, bf16[256,256]{1,0:T(8,128)(2,1)}, u32[]{:S(2)}) copy-start(bf16[256,256]{1,0:T(8,128)(2,1)} %self_second.1) | copy-start | bytes 393220
  2.2 1.8 copy-start
  2.2 1.8 copy-start.1
  2.4 1.7 copy-start.4
  2.4 1.7 copy-start.5
  2.4 1.7 copy-start.6
  2.4 1.7 copy-start.7
  4.1 0.9 copy-start.3
  181.4 1.1 copy-start.9
  182.6 1.2 copy-start.8

commit v2 on v1

v2 whole, which is shorter than its diff:
```python
import functools

import jax
import jax.numpy as jnp
from jax import lax
from jax.experimental import pallas as pl
from jax.experimental.pallas import tpu as pltpu
from jax.sharding import PartitionSpec as P

MESH = pl.DeviceIdType.MESH
BF = jnp.bfloat16
F32 = jnp.float32
CHUNK = 256
TRAVEL = jnp.bfloat16
LOAD_ORDER = (7, 9, 11, 0, 2, 8, 10, 12, 13, 1, 3, 4, 5, 6)


def nn(a, b):
    return lax.dot_general(a, b, (((1,), (0,)), ((), ())), preferred_element_type=F32)


def nt(a, b):
    return lax.dot_general(a, b, (((1,), (1,)), ((), ())), preferred_element_type=F32)


def split(value):
    high = value.astype(BF)
    low = (value - high.astype(F32)).astype(BF)
    return high, low


def blocks(total, step, body):
    def one(i, carry):
        body(pl.ds(pl.multiple_of(i * step, step), step), i * step)
        return carry

    lax.fori_loop(0, total // step, one, 0)


def one_if(flag):
    return jnp.where(flag, 1.0, 0.0).astype(BF)


def kernel(
    peers,
    *refs,
):
    arguments, refs = refs[:14], refs[14:]
    held, refs = refs[3:17], refs[:3] + refs[17:]
    step_through(peers, arguments, held, *refs)


def step_through(
    peers,
    arguments,
    held,
    out_embedding,
    out_gradients,
    out_bias,
    embedding,
    bias_total,
    out_sems,
    held_sems,
    ask_send,
    ask_recv,
    asked,
    a1,
    a1t,
    a2,
    a2t,
    p1,
    p2,
    p2t,
    p3,
    p3t,
    source_t,
    source,
    target_t,
    target,
    features_t,
    arrived_t,
    hidden_t,
    inv1,
    inv2,
    base,
    before,
    hidden,
    left,
    grad,
    own,
    totals,
    slot_first,
    sends,
    recvs,
    highs,
    lows,
    feature_send,
    feature_recv,
    bias_send,
    bias_near,
    bias_held,
    bias_recv,
    gradients,
    pair_send,
    pair_recv,
    shard_send,
    shard_recv,
    final,
    send_sems,
    recv_sems,
):
    me = lax.axis_index("coop")
    loads = [
        pltpu.make_async_copy(argument, place, held_sems.at[n])
        for n, (argument, place) in enumerate(zip(arguments, held))
    ]
    for n in LOAD_ORDER:
        loads[n].start()
    (
        features,
        self_first,
        neighbour_first,
        bias_first,
        self_second,
        neighbour_second,
        bias_second,
        request_first,
        adjacent_first,
        request_second,
        adjacent_second,
        request_edges,
        edge_source,
        edge_target,
    ) = held
    chip = me // 2
    core = me % 2
    chips = peers // 2
    nodes, width = hidden.shape
    feats = features.shape[1]
    slots = a1.shape[1]
    edges = edge_source.shape[1]
    cap = slots // peers
    step = min(CHUNK, slots)

    barrier = pltpu.get_barrier_semaphore()

    def greet(k, carry):
        pl.semaphore_signal(
            barrier, inc=1, device_id={"coop": (me + k) % peers}, device_id_type=MESH
        )
        return carry

    lax.fori_loop(1, peers, greet, 0)

    def count(adjacent, matrix_t):
        tall = 32
        table = adjacent[...]

        def fill(rows, start):
            slot = lax.broadcasted_iota(jnp.int32, (tall, nodes), 0) + start
            total = jnp.zeros((tall, nodes), F32)
            for j in range(table.shape[0]):
                total = total + jnp.where(table[j : j + 1, :] == slot, 1.0, 0.0)
            matrix_t[rows, :] = total.astype(BF)

        blocks(slots, tall, fill)

    def transpose(src, dst):
        def one(rows, start):
            shape = (128, src.shape[1])
            row = lax.broadcasted_iota(jnp.int32, shape, 0) + start
            dst[rows, :] = nt(
                one_if(row == lax.broadcasted_iota(jnp.int32, shape, 1)), src[...]
            ).astype(BF)

        blocks(src.shape[1], 128, one)

    def inverse(matrix, result):
        def one(rows, start):
            result[rows, :] = 1.0 / nn(matrix[rows, :], jnp.ones((slots, width), BF))

        blocks(nodes, CHUNK, one)

    for n in LOAD_ORDER[:7]:
        loads[n].wait()
    for n, request in enumerate((request_first, request_second, request_edges)):
        wanted = request[...].T
        for d in range(peers):
            ask_send[d, :, cap * n : cap * (n + 1)] = wanted[d : d + 1, :]

    def project_first(rows, start):
        left[rows, :] = nn(features[rows, :], neighbour_first[...]).astype(BF)

    blocks(nodes, CHUNK, project_first)
    count(adjacent_first, a1t)
    count(adjacent_second, a2t)
    for n in LOAD_ORDER[7:]:
        loads[n].wait()
    vertex = lax.broadcasted_iota(jnp.int32, (nodes, edges), 0)
    source_t[...] = one_if(vertex == edge_source[...])
    slot = lax.broadcasted_iota(jnp.int32, (slots, edges), 0)
    target_t[...] = one_if(slot == edge_target[...])

    pl.semaphore_wait(barrier, peers - 1)

    def ask(k, carry):
        peer = (me + k) % peers
        pltpu.make_async_remote_copy(
            ask_send.at[peer],
            ask_recv.at[me],
            send_sems.at[10],
            recv_sems.at[10],
            device_id={"coop": peer},
            device_id_type=MESH,
        ).start()
        return carry

    lax.fori_loop(1, peers, ask, 0)
    ask_recv[pl.ds(me, 1)] = ask_send[pl.ds(me, 1)]

    def base_first(rows, start):
        base[rows, :] = nn(features[rows, :], self_first[...]) + bias_first[...]

    blocks(nodes, CHUNK, base_first)
    transpose(a1t, a1)
    inverse(a1, inv1)

    others = pl.ds(0, peers - 1)
    pltpu.make_async_copy(ask_recv.at[others], ask_recv.at[others], recv_sems.at[10]).wait()
    for d in range(peers):
        asked[d : d + 1, :] = ask_recv[d]

    def mine(n, start):
        table = asked[...]
        low = table % 16
        parts = jnp.concatenate([table - low, low], axis=1).astype(F32).astype(BF)
        row = lax.broadcasted_iota(jnp.int32, (step, peers), 0) + start
        owner = lax.broadcasted_iota(jnp.int32, (step, peers), 1)
        spread = nn(one_if(row // cap == owner), parts)
        row = lax.broadcasted_iota(jnp.int32, spread.shape, 0) + start
        lane = lax.broadcasted_iota(jnp.int32, spread.shape, 1) % 128
        return jnp.where(lane == n * cap + row % cap, spread, 0.0).astype(BF)

    def picks(n, matrix):
        def one(rows, start):
            part = mine(n, start)
            wanted = nt(part, jnp.ones((nodes, part.shape[1]), BF))
            matrix[rows, :] = one_if(
                wanted == lax.broadcasted_iota(jnp.int32, wanted.shape, 1).astype(F32)
            )

        blocks(slots, step, one)

    def picks_t(n, matrix):
        def one(rows, start):
            part = mine(n, start)
            wanted = nt(jnp.ones((nodes, part.shape[1]), BF), part)
            matrix[:, rows] = one_if(
                wanted == lax.broadcasted_iota(jnp.int32, wanted.shape, 0).astype(F32)
            )

        blocks(slots, step, one)

    def exchange(phase, side):
        def send(k, carry):
            peer = (me + k) % peers
            pltpu.make_async_remote_copy(
                sends.at[phase, side, pl.ds(pl.multiple_of(peer * cap, cap), cap)],
                recvs.at[phase, side, pl.ds(pl.multiple_of(me * cap, cap), cap)],
                send_sems.at[2 * phase + side],
                recv_sems.at[2 * phase + side],
                device_id={"coop": peer},
                device_id_type=MESH,
            ).start()
            return carry

        lax.fori_loop(1, peers, send, 0)
        mine = pl.ds(pl.multiple_of(me * cap, cap), cap)
        recvs[phase, side, mine, :] = sends[phase, side, mine, :]

    def sent(phase, side):
        most = sends.at[phase, side, pl.ds(0, (peers - 1) * cap)]
        pltpu.make_async_copy(most, most, send_sems.at[2 * phase + side]).wait()

    def arrived(phase, side):
        most = recvs.at[phase, side, pl.ds(0, (peers - 1) * cap)]
        pltpu.make_async_copy(most, most, recv_sems.at[2 * phase + side]).wait()

    def send_features(part):
        def send(k, carry):
            peer = (me + 4 * k + part) % peers
            pltpu.make_async_remote_copy(
                feature_send.at[pl.ds(pl.multiple_of(peer * cap, cap), cap)],
                feature_recv.at[pl.ds(pl.multiple_of(me * cap, cap), cap)],
                send_sems.at[11],
                recv_sems.at[11],
                device_id={"coop": peer},
                device_id_type=MESH,
            ).start()
            return carry

        lax.fori_loop(1 if part == 0 else 0, peers // 4, send, 0)

    half = width // 2
    sides = (slice(0, half), slice(half, width))

    def fill(phase, matrix, rows_of):
        def one(rows, start):
            part = nn(matrix[rows, :], rows_of[...]).astype(BF)
            for side in range(2):
                sends[phase, side, rows, :] = part[:, sides[side]]

        blocks(slots, step, one)
        for side in range(2):
            exchange(phase, side)

    def fill_side(phase, side, matrix, *pieces):
        def one(rows, start):
            part = matrix[rows, :]
            total = nn(part, pieces[0])
            for piece in pieces[1:]:
                total = total + nn(part, piece)
            sends[phase, side, rows, :] = total.astype(BF)

        blocks(slots, step, one)
        exchange(phase, side)

    picks(0, p1)
    fill(0, p1, left)

    def gather_features(rows, start):
        feature_send[rows, :] = nn(p1[rows, :], features[...]).astype(BF)

    blocks(slots, step, gather_features)
    here = pl.ds(pl.multiple_of(me * cap, cap), cap)
    feature_recv[here, :] = feature_send[here, :]
    picks(1, p2)
    sent(0, 0)
    sent(0, 1)
    send_features(0)
    for side in range(2):
        arrived(0, side)
        cols = sides[side]

        def layer_one(rows, start):
            value = base[rows, cols] + nn(a1[rows, :], recvs[0, side]) * inv1[rows, cols]
            before[rows, cols] = value
            part = jnp.maximum(value, 0.0).astype(BF)
            hidden[rows, cols] = part
            more = nn(part, neighbour_second[cols, :])
            if side == 0:
                totals[rows, :] = more
            else:
                left[rows, :] = (totals[rows, :] + more).astype(BF)

        blocks(nodes, CHUNK, layer_one)

    fill(1, p2, left)

    def second_base(rows, start):
        base[rows, :] = nn(hidden[rows, :], self_second[...]) + bias_second[...]

    blocks(nodes, CHUNK, second_base)
    transpose(a2t, a2)
    inverse(a2, inv2)
    picks(2, p3)
    for side in range(2):
        arrived(1, side)
        cols = sides[side]

        def layer_two(rows, start):
            embedding[rows, cols] = (
                base[rows, cols] + nn(a2[rows, :], recvs[1, side]) * inv2[rows, cols]
            ).astype(BF)

        blocks(nodes, CHUNK, layer_two)
        fill_side(2, side, p3, embedding[:, cols])
    leave = [
        pltpu.make_async_copy(embedding, out_embedding, out_sems.at[0]),
        pltpu.make_async_copy(bias_total, out_bias, out_sems.at[1]),
        pltpu.make_async_copy(final, out_gradients, out_sems.at[2]),
    ]
    leave[0].start()
    transpose(source_t, source)
    transpose(target_t, target)

    def lefts(rows, start):
        left[rows, :] = nn(source[rows, :], embedding[...]).astype(BF)

    blocks(edges, CHUNK, lefts)
    transpose(hidden, hidden_t)
    picks_t(2, p3t)
    for side in range(2):
        sent(1, side)
        sent(2, side)
    send_features(1)
    arrived(2, 0)

    def first_scores(rows, start):
        right = nn(target[rows, :], recvs[2, 0])
        own[rows, sides[0]] = right
        grad[rows, sides[0]] = left[rows, sides[0]].astype(F32) * right

    blocks(edges, CHUNK, first_scores)
    arrived(2, 1)

    def scores(rows, start):
        right = nn(target[rows, :], recvs[2, 1])
        here = left[rows, :].astype(F32)
        products = grad[rows, sides[0]] + here[:, sides[1]] * right
        score = jnp.sum(products, axis=1, keepdims=True) * width ** (-0.5)
        edge = lax.broadcasted_iota(jnp.int32, score.shape, 0) + start
        label = jnp.where(edge < edges // 2, 1.0, 0.0)
        coef = (jax.nn.sigmoid(score) - label) * (edges * peers * width) ** (-0.5)
        grad[rows, :] = coef * here
        own[rows, sides[0]] = coef * own[rows, sides[0]]
        own[rows, sides[1]] = coef * right

    blocks(edges, CHUNK, scores)
    for side in range(2):
        fill_side(3, side, target_t, *split(grad[:, sides[side]]))
    high, low = split(own[...])
    totals[...] = nn(source_t[...], high) + nn(source_t[...], low)
    picks_t(1, p2t)
    transpose(features, features_t)
    sent(3, 0)
    sent(3, 1)
    send_features(2)
    for side in range(2):
        arrived(3, side)
        cols = sides[side]

        def outer(rows, start):
            grad[rows, cols] = totals[rows, cols] + nn(p3t[rows, :], recvs[3, side])

        blocks(nodes, CHUNK, outer)
        fill_side(4, side, a2t, *split(grad[:, cols] * inv2[:, cols]))
    send_features(3)
    bias_send[:, :, :width] = jnp.sum(grad[...], axis=0, keepdims=True)[None]
    outer_round = grad[...].astype(BF)
    second = slice(half, half + width)
    gradients[1, :width, second] = nn(hidden_t[...], outer_round)
    own[...] = nt(outer_round, self_second[...])
    for side in range(2):
        arrived(4, side)
        cols = sides[side]

        def second_totals(rows, start):
            value = nn(p2t[rows, :], recvs[4, side])
            high, low = split(value)
            highs[rows, cols] = high
            lows[rows, cols] = low
            weight = neighbour_second[:, cols]
            value = own[rows, :] + nt(high, weight) + nt(low, weight)
            if side == 0:
                own[rows, :] = value
            else:
                grad[rows, :] = jnp.where(before[rows, :] > 0.0, value, 0.0)

        blocks(nodes, CHUNK, second_totals)

    most = feature_recv.at[pl.ds(0, (peers - 1) * cap)]
    pltpu.make_async_copy(most, most, recv_sems.at[11]).wait()
    transpose(feature_recv, arrived_t)
    inner_round = grad[...].astype(BF)
    high, low = split(grad[...] * inv1[...])

    def slot_totals(rows, start):
        part = a1t[rows, :]
        slot_first[rows, :] = (nn(part, high) + nn(part, low)).astype(BF)

    blocks(slots, step, slot_totals)

    def first_gradients(rows, start):
        gradients[0, rows, :width] = nn(features_t[rows, :], inner_round)
        near = nn(arrived_t[rows, :], slot_first[...])
        gradients[0, rows, width:] = near[:, :half]
        gradients[1, rows, :half] = near[:, half:]

    blocks(feats, CHUNK, first_gradients)
    gradients[1, width:, second] = nn(hidden_t[...], highs[...]) + nn(hidden_t[...], lows[...])
    bias_send[:, :, width:] = jnp.sum(grad[...], axis=0, keepdims=True)[None]

    share = feats // chips
    partner = chip * 2 + 1 - core
    pair_send[...] = gradients[1 - core].astype(pair_send.dtype)
    pair = pltpu.make_async_remote_copy(
        pair_send,
        pair_recv,
        send_sems.at[13],
        recv_sems.at[13],
        device_id={"coop": partner},
        device_id_type=MESH,
    )
    pair.start()
    bias_pair = pltpu.make_async_remote_copy(
        bias_send,
        bias_near,
        send_sems.at[12],
        recv_sems.at[12],
        device_id={"coop": partner},
        device_id_type=MESH,
    )
    bias_pair.start()
    pair.wait_recv()
    shard_send[...] = (gradients[core] + pair_recv[...].astype(F32)).astype(shard_send.dtype)

    def scatter(k, carry):
        to = (chip + k) % chips
        pltpu.make_async_remote_copy(
            shard_send.at[pl.ds(pl.multiple_of(to * share, share), share)],
            shard_recv.at[pl.ds(pl.multiple_of(chip * share, share), share)],
            send_sems.at[14],
            recv_sems.at[14],
            device_id={"coop": to * 2 + core},
            device_id_type=MESH,
        ).start()
        return carry

    lax.fori_loop(1, chips, scatter, 0)
    place = pl.ds(pl.multiple_of(chip * share, share), share)
    shard_recv[place, :] = shard_send[place, :]
    bias_pair.wait_recv()
    bias_held[...] = bias_send[...] + bias_near[...]

    def spread_bias(k, carry):
        to = (chip + k) % chips
        pltpu.make_async_remote_copy(
            bias_held.at[0],
            bias_recv.at[chip],
            send_sems.at[17],
            recv_sems.at[17],
            device_id={"coop": to * 2 + core},
            device_id_type=MESH,
        ).start()
        return carry

    lax.fori_loop(1, chips, spread_bias, 0)
    bias_recv[pl.ds(chip, 1)] = bias_held[...]
    most = shard_recv.at[pl.ds(0, (chips - 1) * share)]
    pltpu.make_async_copy(most, most, recv_sems.at[14]).wait()
    total = shard_recv[0:share, :].astype(F32)
    for c in range(1, chips):
        total = total + shard_recv[c * share : (c + 1) * share, :].astype(F32)
    final[core, place, :] = total.astype(final.dtype)

    def gather(k, carry):
        to = (chip + k) % chips
        pltpu.make_async_remote_copy(
            final.at[core, place],
            final.at[core, place],
            send_sems.at[15],
            recv_sems.at[15],
            device_id={"coop": to * 2 + core},
            device_id_type=MESH,
        ).start()
        return carry

    lax.fori_loop(1, chips, gather, 0)
    far = pl.ds(0, chips - 1)
    pltpu.make_async_copy(bias_recv.at[far], bias_recv.at[far], recv_sems.at[17]).wait()
    total = bias_recv[0]
    for c in range(1, chips):
        total = total + bias_recv[c]
    bias_total[...] = total
    leave[1].start()
    pltpu.make_async_copy(most, most, recv_sems.at[15]).wait()
    back = pltpu.make_async_remote_copy(
        final.at[core],
        final.at[core],
        send_sems.at[16],
        recv_sems.at[16],
        device_id={"coop": partner},
        device_id_type=MESH,
    )
    back.start()
    back.wait_recv()
    leave[2].start()

    sent(4, 0)
    sent(4, 1)
    pltpu.make_async_copy(ask_send.at[others], ask_send.at[others], send_sems.at[10]).wait()
    gone = feature_send.at[pl.ds(0, (peers - 1) * cap)]
    pltpu.make_async_copy(gone, gone, send_sems.at[11]).wait()
    bias_pair.wait_send()
    pltpu.make_async_copy(bias_recv.at[far], bias_recv.at[far], send_sems.at[17]).wait()
    pair.wait_send()
    pltpu.make_async_copy(most, most, send_sems.at[14]).wait()
    pltpu.make_async_copy(most, most, send_sems.at[15]).wait()
    back.wait_send()
    for copy in leave:
        copy.wait()


def finish(
    in_embedding,
    in_gradients,
    in_bias,
    out_embedding,
    out_self_first,
    out_neighbour_first,
    out_bias_first,
    out_self_second,
    out_neighbour_second,
    out_bias_second,
    embedding,
    bias,
    self_first,
    neighbour_first,
    self_second,
    neighbour_second,
    gradients,
    sems,
):
    loads = [
        pltpu.make_async_copy(in_gradients, gradients, sems.at[7]),
        pltpu.make_async_copy(in_embedding, embedding, sems.at[8]),
        pltpu.make_async_copy(in_bias, bias, sems.at[9]),
    ]
    for load in loads:
        load.start()
    width = embedding.shape[1]
    edge = width // 2
    copies = []

    def leave(src, dst):
        copies.append(pltpu.make_async_copy(src, dst, sems.at[len(copies)]))
        copies[-1].start()

    loads[0].wait()
    self_first[...] = gradients[0, :, :width].astype(F32)
    leave(self_first, out_self_first)
    neighbour_first[:, :edge] = gradients[0, :, width:].astype(F32)
    neighbour_first[:, edge:] = gradients[1, :, :edge].astype(F32)
    leave(neighbour_first, out_neighbour_first)
    loads[1].wait()
    leave(embedding, out_embedding)
    self_second[...] = gradients[1, :width, edge:].astype(F32)
    leave(self_second, out_self_second)
    neighbour_second[...] = gradients[1, width:, edge:].astype(F32)
    leave(neighbour_second, out_neighbour_second)
    loads[2].wait()
    leave(bias.at[:, :width], out_bias_second)
    leave(bias.at[:, width:], out_bias_first)
    for copy in copies:
        copy.wait()


def per_device(
    features,
    self_first,
    neighbour_first,
    bias_first,
    self_second,
    neighbour_second,
    bias_second,
    request_first,
    adjacent_first,
    request_second,
    adjacent_second,
    request_edges,
    edge_source,
    edge_target,
):
    nodes, feats = features.shape
    width = self_first.shape[1]
    _, peers, cap = request_first.shape
    slots = peers * cap
    edges = edge_source.shape[0]
    wide = 3 * width // 2
    arguments = (
        features,
        self_first,
        neighbour_first,
        bias_first.reshape(1, width),
        self_second,
        neighbour_second,
        bias_second.reshape(1, width),
        request_first[0].T,
        adjacent_first.T,
        request_second[0].T,
        adjacent_second.T,
        request_edges[0].T,
        edge_source.reshape(1, edges),
        edge_target.reshape(1, edges),
    )
    vmem = pltpu.VMEM
    scratch = [vmem(a.shape, a.dtype) for a in arguments] + [
        vmem((nodes, width), BF),
        vmem((1, 2 * width), F32),
        pltpu.SemaphoreType.DMA((3,)),
        pltpu.SemaphoreType.DMA((14,)),
        vmem((peers, 1, 128), jnp.int32),
        vmem((peers, 1, 128), jnp.int32),
        vmem((peers, 128), jnp.int32),
        vmem((nodes, slots), BF),
        vmem((slots, nodes), BF),
        vmem((nodes, slots), BF),
        vmem((slots, nodes), BF),
        vmem((slots, nodes), BF),
        vmem((slots, nodes), BF),
        vmem((nodes, slots), BF),
        vmem((slots, nodes), BF),
        vmem((nodes, slots), BF),
        vmem((nodes, edges), BF),
        vmem((edges, nodes), BF),
        vmem((slots, edges), BF),
        vmem((edges, slots), BF),
        vmem((feats, nodes), BF),
        vmem((feats, slots), BF),
        vmem((width, nodes), BF),
        vmem((nodes, width), F32),
        vmem((nodes, width), F32),
        vmem((nodes, width), F32),
        vmem((nodes, width), F32),
        vmem((nodes, width), BF),
        vmem((nodes, width), BF),
        vmem((nodes, width), F32),
        vmem((nodes, width), F32),
        vmem((nodes, width), F32),
        vmem((slots, width), BF),
        vmem((5, 2, slots, width // 2), BF),
        vmem((5, 2, slots, width // 2), BF),
        vmem((nodes, width), BF),
        vmem((nodes, width), BF),
        vmem((slots, feats), BF),
        vmem((slots, feats), BF),
        vmem((1, 1, 2 * width), F32),
        vmem((1, 1, 2 * width), F32),
        vmem((1, 1, 2 * width), F32),
        vmem((peers // 2, 1, 2 * width), F32),
        vmem((2, feats, wide), F32),
        vmem((feats, wide), TRAVEL),
        vmem((feats, wide), TRAVEL),
        vmem((feats, wide), TRAVEL),
        vmem((feats, wide), TRAVEL),
        vmem((2, feats, wide), TRAVEL),
        pltpu.SemaphoreType.DMA((18,)),
        pltpu.SemaphoreType.DMA((18,)),
    ]
    summed = pl.pallas_call(
        functools.partial(kernel, peers),
        out_shape=(
            jax.ShapeDtypeStruct((nodes, width), BF),
            jax.ShapeDtypeStruct((2, feats, wide), TRAVEL),
            jax.ShapeDtypeStruct((1, 2 * width), F32),
        ),
        in_specs=[pl.BlockSpec(memory_space=pltpu.HBM)] * 14,
        out_specs=[pl.BlockSpec(memory_space=pltpu.HBM)] * 3,
        scratch_shapes=scratch,
        compiler_params=pltpu.CompilerParams(
            collective_id=0, has_side_effects=True, vmem_limit_bytes=60 * 2**20
        ),
    )(*arguments)
    results = pl.pallas_call(
        finish,
        out_shape=(
            jax.ShapeDtypeStruct((nodes, width), BF),
            jax.ShapeDtypeStruct((feats, width), F32),
            jax.ShapeDtypeStruct((feats, width), F32),
            jax.ShapeDtypeStruct((1, width), F32),
            jax.ShapeDtypeStruct((width, width), F32),
            jax.ShapeDtypeStruct((width, width), F32),
            jax.ShapeDtypeStruct((1, width), F32),
        ),
        in_specs=[pl.BlockSpec(memory_space=pltpu.HBM)] * 3,
        out_specs=[pl.BlockSpec(memory_space=pltpu.HBM)] * 7,
        scratch_shapes=[
            vmem((nodes, width), BF),
            vmem((1, 2 * width), F32),
            vmem((feats, width), F32),
            vmem((feats, width), F32),
            vmem((width, width), F32),
            vmem((width, width), F32),
            vmem((2, feats, wide), TRAVEL),
            pltpu.SemaphoreType.DMA((10,)),
        ],
        compiler_params=pltpu.CompilerParams(vmem_limit_bytes=60 * 2**20),
    )(*summed)
    return (
        results[0],
        results[1],
        results[2],
        results[3].reshape(width),
        results[4],
        results[5],
        results[6].reshape(width),
    )


def solution(mesh):
    in_specs = (
        P(("dp", "coop"), None),
        P(),
        P(),
        P(),
        P(),
        P(),
        P(),
        P(("dp", "coop"), None, None),
        P(("dp", "coop"), None),
        P(("dp", "coop"), None, None),
        P(("dp", "coop"), None),
        P(("dp", "coop"), None, None),
        P(("dp", "coop")),
        P(("dp", "coop")),
    )
    out_specs = (
        P(("dp", "coop"), None),
        P("dp", None),
        P("dp", None),
        P("dp"),
        P("dp", None),
        P("dp", None),
        P("dp"),
    )
    return jax.shard_map(
        per_device, mesh=mesh, in_specs=in_specs, out_specs=out_specs, check_vma=False
    )
```

time: 187 us -> 142 us (0.76)
  Pallas kernels: 176 us -> 141 us
  local copies, waits for them, and re-layouts: 9.94 us -> 0 us
    pallas_call x1, Pallas kernels: 176 us -> 138 us  [per_device(): pl.pallas_call(functools.partial(kernel, peers), out_shape=(jax.ShapeDtyp...]
    unnamed x38 -> x0, local copies, waits for them, and re-layouts: 9.94 us -> none
    pallas_call x0 -> x1, Pallas kernels: none -> 2.48 us  [per_device(): pl.pallas_call(finish, out_shape=(jax.ShapeDtypeStruct((nodes, width), BF...]
where the time goes in v2:
time: 142 us
  Pallas kernels  141 us (99%)
    pallas_call x1, Pallas kernels, per_device(): pl.pallas_call(functools.partial(kernel, peers), out_shape=(jax.ShapeDtyp...  138 us

profile of v2, /device:TPU:1, one launch (start us, length us, event | category | flops | bytes accessed | tf_op | source)
XLA Modules:
  0.0 141.6 jit_solution(14073380264571517020)
XLA Ops:
  0.6 138.5 %shard_map.189 = (bf16[512,256]{1,0:T(8,128)(2,1)}, bf16[2,512,384]{2,1,0:T(8,128)(2,1)}, f32[1,512]{1,0:T(1,128)}) custom-call(bf16[512,512]{1,0:T(8,128)(2,1)} %refs_0_.1, bf16[512,256]{1,0:T(8,128)(2,1)} %refs_1_.1, bf16[512,256]{1,0:T(8,128)(2,1)} %refs_2_.1, f32[1,256]{1,0:T(1,128)} %bitcast.24, bf16[256,256]{1,0:T(8,128)(2,1)} %refs_4_.1, ...), custom_call_target="tpu_custom_call" | custom-call | tf_op jit(solution)/shard_map/pallas_call | solution.py:741
  139.1 2.5 %shard_map.190 = (bf16[512,256]{1,0:T(8,128)(2,1)}, f32[512,256]{1,0:T(8,128)}, f32[512,256]{1,0:T(8,128)}, f32[1,256]{1,0:T(1,128)}, f32[256,256]{1,0:T(8,128)}, /*index=5*/f32[256,256]{1,0:T(8,128)}, f32[1,256]{1,0:T(1,128)}) custom-call(bf16[512,256]{1,0:T(8,128)(2,1)} %get-tuple-element.17.in_embedding, ...), custom_call_target="tpu_custom_call" | custom-call | tf_op jit(solution)/shard_map/pallas_call | solution.py:755

commit v3 on v2

v3 whole, which is shorter than its diff:
```python
import functools

import jax
import jax.numpy as jnp
from jax import lax
from jax.experimental import pallas as pl
from jax.experimental.pallas import tpu as pltpu
from jax.sharding import PartitionSpec as P

MESH = pl.DeviceIdType.MESH
BF = jnp.bfloat16
F32 = jnp.float32
CHUNK = 256
XS = 4
ZS = 8
TRAVEL = jnp.bfloat16
LOAD_ORDER = (7, 9, 11, 0, 2, 8, 10, 12, 13, 1, 3, 4, 5, 6)


def far_x(i):
    return (1 - i // 2) * (2 + i) + (i // 2) * (3 - i)


def far_z(j):
    return ZS // 2 + (j // 2) * (1 - 2 * (j % 2)) - j % 2


def every(body):
    def one(n, carry):
        body(far_x(n // ZS), far_z(n % ZS))
        return carry

    lax.fori_loop(0, XS * ZS, one, 0)


def nn(a, b):
    return lax.dot_general(a, b, (((1,), (0,)), ((), ())), preferred_element_type=F32)


def nt(a, b):
    return lax.dot_general(a, b, (((1,), (1,)), ((), ())), preferred_element_type=F32)


def split(value):
    high = value.astype(BF)
    low = (value - high.astype(F32)).astype(BF)
    return high, low


def blocks(total, step, body):
    def one(i, carry):
        body(pl.ds(pl.multiple_of(i * step, step), step), i * step)
        return carry

    lax.fori_loop(0, total // step, one, 0)


def one_if(flag):
    return jnp.where(flag, 1.0, 0.0).astype(BF)


def kernel(
    peers,
    *refs,
):
    arguments, refs = refs[:14], refs[14:]
    held, refs = refs[4:18], refs[:4] + refs[18:]
    step_through(peers, arguments, held, *refs)


def step_through(
    peers,
    arguments,
    held,
    out_embedding,
    out_one,
    out_two,
    out_bias,
    embedding,
    bias_total,
    out_sems,
    held_sems,
    ask_send,
    ask_recv,
    asked,
    a1,
    a1t,
    a2,
    a2t,
    p1,
    p1t,
    p2,
    p2t,
    p3,
    p3t,
    source_t,
    source,
    target_t,
    target,
    features_t,
    hidden_t,
    inv1,
    inv2,
    base,
    before,
    hidden,
    left,
    grad,
    own,
    totals,
    sends,
    recvs,
    highs,
    lows,
    bias_send,
    bias_near,
    bias_held,
    bias_recv,
    grads_one,
    pair_one,
    shards_one,
    final_one,
    grads_two,
    pair_two,
    shards_two,
    final_two,
    send_sems,
    recv_sems,
):
    me = lax.axis_index("coop")
    chip = me // 2
    core = me % 2
    chips = peers // 2
    barrier = pltpu.get_barrier_semaphore()

    def chip_at(x, z):
        return (chip // ZS + x) % XS * ZS + (chip + z) % ZS

    def to_all(start):
        def both(x, z):
            to = chip_at(x, z) * 2
            start(to + 1 - core)

            @pl.when(to + core != me)
            def _():
                start(to + core)

        every(both)

    def to_others(start):
        def one(x, z):
            to = chip_at(x, z)

            @pl.when(to != chip)
            def _():
                start(to)

        every(one)

    def greet(peer):
        pl.semaphore_signal(barrier, inc=1, device_id={"coop": peer}, device_id_type=MESH)

    to_all(greet)
    loads = [
        pltpu.make_async_copy(argument, place, held_sems.at[n])
        for n, (argument, place) in enumerate(zip(arguments, held))
    ]
    for n in LOAD_ORDER:
        loads[n].start()
    (
        features,
        self_first,
        neighbour_first,
        bias_first,
        self_second,
        neighbour_second,
        bias_second,
        request_first,
        adjacent_first,
        request_second,
        adjacent_second,
        request_edges,
        edge_source,
        edge_target,
    ) = held
    nodes, width = hidden.shape
    feats = features.shape[1]
    slots = a1.shape[1]
    edges = edge_source.shape[1]
    cap = slots // peers
    step = slots // XS

    def count(adjacent, matrix_t):
        tall = 32
        table = adjacent[...]

        def fill(rows, start):
            slot = lax.broadcasted_iota(jnp.int32, (tall, nodes), 0) + start
            total = jnp.zeros((tall, nodes), F32)
            for j in range(table.shape[0]):
                total = total + jnp.where(table[j : j + 1, :] == slot, 1.0, 0.0)
            matrix_t[rows, :] = total.astype(BF)

        blocks(slots, tall, fill)

    def transpose(src, dst):
        def one(rows, start):
            shape = (128, src.shape[1])
            row = lax.broadcasted_iota(jnp.int32, shape, 0) + start
            dst[rows, :] = nt(
                one_if(row == lax.broadcasted_iota(jnp.int32, shape, 1)), src[...]
            ).astype(BF)

        blocks(src.shape[1], 128, one)

    def inverse(matrix, result):
        def one(rows, start):
            result[rows, :] = 1.0 / nn(matrix[rows, :], jnp.ones((slots, width), BF))

        blocks(nodes, CHUNK, one)

    for n in LOAD_ORDER[:5]:
        loads[n].wait()
    for n, request in enumerate((request_first, request_second, request_edges)):
        wanted = request[...].T
        for d in range(peers):
            ask_send[d, :, cap * n : cap * (n + 1)] = wanted[d : d + 1, :]

    def project_first(rows, start):
        left[rows, :] = nn(features[rows, :], neighbour_first[...]).astype(BF)

    blocks(nodes, CHUNK, project_first)
    for n in LOAD_ORDER[5:]:
        loads[n].wait()

    pl.semaphore_wait(barrier, peers - 1)

    def ask(peer):
        pltpu.make_async_remote_copy(
            ask_send.at[peer],
            ask_recv.at[me],
            send_sems.at[15],
            recv_sems.at[15],
            device_id={"coop": peer},
            device_id_type=MESH,
        ).start()

    to_all(ask)
    ask_recv[pl.ds(me, 1)] = ask_send[pl.ds(me, 1)]

    def base_first(rows, start):
        base[rows, :] = nn(features[rows, :], self_first[...]) + bias_first[...]

    blocks(nodes, CHUNK, base_first)
    count(adjacent_first, a1t)

    others = pl.ds(0, peers - 1)
    pltpu.make_async_copy(ask_recv.at[others], ask_recv.at[others], recv_sems.at[15]).wait()
    for d in range(peers):
        asked[d : d + 1, :] = ask_recv[d]

    def mine(n, start):
        table = asked[...]
        low = table % 16
        parts = jnp.concatenate([table - low, low], axis=1).astype(F32).astype(BF)
        row = lax.broadcasted_iota(jnp.int32, (step, peers), 0) + start
        owner = lax.broadcasted_iota(jnp.int32, (step, peers), 1)
        spread = nn(one_if(row // cap == owner), parts)
        row = lax.broadcasted_iota(jnp.int32, spread.shape, 0) + start
        lane = lax.broadcasted_iota(jnp.int32, spread.shape, 1) % 128
        return jnp.where(lane == n * cap + row % cap, spread, 0.0).astype(BF)

    def picks(n, matrix):
        def one(rows, start):
            part = mine(n, start)
            wanted = nt(part, jnp.ones((nodes, part.shape[1]), BF))
            matrix[rows, :] = one_if(
                wanted == lax.broadcasted_iota(jnp.int32, wanted.shape, 1).astype(F32)
            )

        blocks(slots, step, one)

    def picks_t(n, matrix):
        def one(rows, start):
            part = mine(n, start)
            wanted = nt(jnp.ones((nodes, part.shape[1]), BF), part)
            matrix[:, rows] = one_if(
                wanted == lax.broadcasted_iota(jnp.int32, wanted.shape, 0).astype(F32)
            )

        blocks(slots, step, one)

    def block(phase, side, peer):
        return pltpu.make_async_remote_copy(
            sends.at[phase, side, pl.ds(pl.multiple_of(peer * cap, cap), cap)],
            recvs.at[phase, side, pl.ds(pl.multiple_of(me * cap, cap), cap)],
            send_sems.at[2 * phase + side],
            recv_sems.at[2 * phase + side],
            device_id={"coop": peer},
            device_id_type=MESH,
        )

    group = 2 * ZS

    def ship(phase, side, body):
        def one(i, carry):
            x = (chip // ZS + far_x(i)) % XS
            start = x * step
            if body is not None:
                body(pl.ds(pl.multiple_of(start, step), step), start)

            def send(j, carry):
                to = x * group + (chip + far_z(j)) % ZS * 2
                block(phase, side, to + 1 - core).start()

                @pl.when(to + core != me)
                def _():
                    block(phase, side, to + core).start()

                return carry

            lax.fori_loop(0, ZS, send, 0)
            return carry

        lax.fori_loop(0, XS, one, 0)
        mine = pl.ds(pl.multiple_of(me * cap, cap), cap)
        recvs[phase, side, mine, :] = sends[phase, side, mine, :]

    def sent(phase, side):
        most = sends.at[phase, side, pl.ds(0, (peers - 1) * cap)]
        pltpu.make_async_copy(most, most, send_sems.at[2 * phase + side]).wait()

    def arrived(phase, side):
        most = recvs.at[phase, side, pl.ds(0, (peers - 1) * cap)]
        pltpu.make_async_copy(most, most, recv_sems.at[2 * phase + side]).wait()

    half = width // 2
    sides = (slice(0, half), slice(half, width))

    def fill(phase, matrix, rows_of):
        def one(rows, start):
            part = nn(matrix[rows, :], rows_of[...]).astype(BF)
            for side in range(2):
                sends[phase, side, rows, :] = part[:, sides[side]]

        ship(phase, 0, one)
        ship(phase, 1, None)

    def fill_side(phase, side, matrix, rows_of):
        def one(rows, start):
            sends[phase, side, rows, :] = nn(matrix[rows, :], rows_of).astype(BF)

        ship(phase, side, one)

    def joined(value):
        return jnp.concatenate(split(value), axis=1)

    def folded(value):
        return value[:, :half] + value[:, half:]

    def fill_split(phase, side, matrix, value):
        pieces = joined(value)

        def one(rows, start):
            sends[phase, side, rows, :] = folded(nn(matrix[rows, :], pieces)).astype(BF)

        ship(phase, side, one)

    picks(0, p1)
    fill(0, p1, left)

    transpose(a1t, a1)
    inverse(a1, inv1)
    picks(1, p2)
    count(adjacent_second, a2t)
    transpose(a2t, a2)
    inverse(a2, inv2)
    picks(2, p3)
    for side in range(2):
        arrived(0, side)
        cols = sides[side]

        def layer_one(rows, start):
            value = base[rows, cols] + nn(a1[rows, :], recvs[0, side]) * inv1[rows, cols]
            before[rows, cols] = value
            part = jnp.maximum(value, 0.0).astype(BF)
            hidden[rows, cols] = part
            more = nn(part, neighbour_second[cols, :])
            if side == 0:
                totals[rows, :] = more
            else:
                left[rows, :] = (totals[rows, :] + more).astype(BF)

        blocks(nodes, CHUNK, layer_one)

    fill(1, p2, left)

    def second_base(rows, start):
        base[rows, :] = nn(hidden[rows, :], self_second[...]) + bias_second[...]

    blocks(nodes, CHUNK, second_base)
    vertex = lax.broadcasted_iota(jnp.int32, (nodes, edges), 0)
    source_t[...] = one_if(vertex == edge_source[...])
    slot = lax.broadcasted_iota(jnp.int32, (slots, edges), 0)
    target_t[...] = one_if(slot == edge_target[...])
    transpose(source_t, source)
    transpose(target_t, target)
    transpose(hidden, hidden_t)
    for side in range(2):
        arrived(1, side)
        cols = sides[side]

        def layer_two(rows, start):
            embedding[rows, cols] = (
                base[rows, cols] + nn(a2[rows, :], recvs[1, side]) * inv2[rows, cols]
            ).astype(BF)

        blocks(nodes, CHUNK, layer_two)
        fill_side(2, side, p3, embedding[:, cols])
    leave = [
        pltpu.make_async_copy(embedding, out_embedding, out_sems.at[0]),
        pltpu.make_async_copy(bias_total, out_bias, out_sems.at[1]),
        pltpu.make_async_copy(final_one, out_one, out_sems.at[2]),
        pltpu.make_async_copy(final_two, out_two, out_sems.at[3]),
    ]
    leave[0].start()

    def lefts(rows, start):
        left[rows, :] = nn(source[rows, :], embedding[...]).astype(BF)

    blocks(edges, CHUNK, lefts)
    picks_t(2, p3t)
    transpose(features, features_t)
    picks_t(1, p2t)
    arrived(2, 0)

    def first_scores(rows, start):
        right = nn(target[rows, :], recvs[2, 0])
        own[rows, sides[0]] = right
        grad[rows, sides[0]] = left[rows, sides[0]].astype(F32) * right

    blocks(edges, CHUNK, first_scores)
    arrived(2, 1)

    def scores(rows, start):
        right = nn(target[rows, :], recvs[2, 1])
        here = left[rows, :].astype(F32)
        products = grad[rows, sides[0]] + here[:, sides[1]] * right
        score = jnp.sum(products, axis=1, keepdims=True) * width ** (-0.5)
        edge = lax.broadcasted_iota(jnp.int32, score.shape, 0) + start
        label = jnp.where(edge < edges // 2, 1.0, 0.0)
        coef = (jax.nn.sigmoid(score) - label) * (edges * peers * width) ** (-0.5)
        grad[rows, :] = coef * here
        own[rows, sides[0]] = coef * own[rows, sides[0]]
        own[rows, sides[1]] = coef * right

    blocks(edges, CHUNK, scores)
    for side in range(2):
        fill_split(3, side, target_t, grad[:, sides[side]])
    high, low = split(own[...])
    totals[...] = nn(source_t[...], high) + nn(source_t[...], low)
    picks_t(0, p1t)
    for side in range(2):
        arrived(3, side)
        cols = sides[side]

        def outer(rows, start):
            grad[rows, cols] = totals[rows, cols] + nn(p3t[rows, :], recvs[3, side])

        blocks(nodes, CHUNK, outer)
        fill_split(4, side, a2t, grad[:, cols] * inv2[:, cols])
    bias_send[:, :, :width] = jnp.sum(grad[...], axis=0, keepdims=True)[None]
    outer_round = grad[...].astype(BF)
    grads_one[1, :width, :] = nn(hidden_t[...], outer_round)
    own[...] = nt(outer_round, self_second[...])
    for side in range(2):
        arrived(4, side)
        cols = sides[side]
        weight = neighbour_second[:, cols]
        weights = jnp.concatenate([weight, weight], axis=1)

        def second_totals(rows, start):
            value = nn(p2t[rows, :], recvs[4, side])
            high, low = split(value)
            highs[rows, cols] = high
            lows[rows, cols] = low
            value = own[rows, :] + nt(jnp.concatenate([high, low], axis=1), weights)
            if side == 0:
                own[rows, :] = value
            else:
                grad[rows, :] = jnp.where(before[rows, :] > 0.0, value, 0.0)

        blocks(nodes, CHUNK, second_totals)

    for side in range(2):
        cols = sides[side]
        fill_split(5, side, a1t, grad[:, cols] * inv1[:, cols])
    inner_round = grad[...].astype(BF)

    def self_gradient(rows, start):
        grads_one[0, rows, :] = nn(features_t[rows, :], inner_round)

    blocks(feats, CHUNK, self_gradient)
    grads_one[1, width:, :] = nn(hidden_t[...], highs[...]) + nn(hidden_t[...], lows[...])

    share = feats // chips
    place = pl.ds(pl.multiple_of(chip * share, share), share)
    partner = chip * 2 + 1 - core

    class Summing:
        def __init__(self, grads, pair, shards, final, first_sem):
            self.grads, self.pair, self.shards, self.final = grads, pair, shards, final
            self.sem = first_sem
            self.swap = self.to_partner(pair.at[0], pair.at[1], 0)
            self.back = self.to_partner(final.at[core], final.at[core], 3)

        def to_partner(self, src, dst, n):
            return pltpu.make_async_remote_copy(
                src,
                dst,
                send_sems.at[self.sem + n],
                recv_sems.at[self.sem + n],
                device_id={"coop": partner},
                device_id_type=MESH,
            )

        def to_chips(self, src_of, dst, n):
            def send(to):
                pltpu.make_async_remote_copy(
                    src_of(to),
                    dst,
                    send_sems.at[self.sem + n],
                    recv_sems.at[self.sem + n],
                    device_id={"coop": to * 2 + core},
                    device_id_type=MESH,
                ).start()

            to_others(send)

        def all_of(self, sem):
            most = self.shards.at[1, pl.ds(0, (chips - 1) * share)]
            pltpu.make_async_copy(most, most, sem).wait()

        def start(self):
            self.pair[0] = self.grads[1 - core].astype(TRAVEL)
            self.swap.start()

        def add_pair(self):
            self.swap.wait_recv()
            self.shards[0] = (self.grads[core] + self.pair[1].astype(F32)).astype(TRAVEL)

        def scatter(self):
            self.to_chips(
                lambda to: self.shards.at[0, pl.ds(pl.multiple_of(to * share, share), share)],
                self.shards.at[1, place],
                1,
            )
            self.shards[1, place, :] = self.shards[0, place, :]

        def gather(self):
            self.all_of(recv_sems.at[self.sem + 1])
            total = self.shards[1, 0:share, :].astype(F32)
            for c in range(1, chips):
                total = total + self.shards[1, c * share : (c + 1) * share, :].astype(F32)
            self.final[core, place, :] = total.astype(TRAVEL)
            mine = self.final.at[core, place]
            self.to_chips(lambda to: mine, mine, 2)

        def give_back(self):
            self.all_of(recv_sems.at[self.sem + 2])
            self.back.start()

        def left(self):
            self.swap.wait_send()
            self.all_of(send_sems.at[self.sem + 1])
            self.all_of(send_sems.at[self.sem + 2])
            self.back.wait_send()

    one = Summing(grads_one, pair_one, shards_one, final_one, 16)
    two = Summing(grads_two, pair_two, shards_two, final_two, 20)
    one.start()
    bias_send[:, :, width:] = jnp.sum(grad[...], axis=0, keepdims=True)[None]
    bias_pair = pltpu.make_async_remote_copy(
        bias_send,
        bias_near,
        send_sems.at[13],
        recv_sems.at[13],
        device_id={"coop": partner},
        device_id_type=MESH,
    )
    bias_pair.start()
    one.add_pair()
    bias_pair.wait_recv()
    bias_held[...] = bias_send[...] + bias_near[...]
    sent(5, 0)
    sent(5, 1)
    one.scatter()

    def spread_bias(to):
        pltpu.make_async_remote_copy(
            bias_held.at[0],
            bias_recv.at[chip],
            send_sems.at[14],
            recv_sems.at[14],
            device_id={"coop": to * 2 + core},
            device_id_type=MESH,
        ).start()

    to_others(spread_bias)
    bias_recv[pl.ds(chip, 1)] = bias_held[...]
    for side in range(2):
        arrived(5, side)
        pieces = joined(nn(p1t[...], recvs[5, side]))

        def near_gradient(rows, start):
            grads_two[side, rows, :] = folded(nn(features_t[rows, :], pieces))

        blocks(feats, CHUNK, near_gradient)
    two.start()
    two.add_pair()
    two.scatter()
    one.gather()
    far = pl.ds(0, chips - 1)
    pltpu.make_async_copy(bias_recv.at[far], bias_recv.at[far], recv_sems.at[14]).wait()
    total = bias_recv[0]
    for c in range(1, chips):
        total = total + bias_recv[c]
    bias_total[...] = total
    leave[1].start()
    two.gather()
    one.give_back()
    two.give_back()
    one.back.wait_recv()
    leave[2].start()
    two.back.wait_recv()
    leave[3].start()

    pltpu.make_async_copy(ask_send.at[others], ask_send.at[others], send_sems.at[15]).wait()
    for phase in range(5):
        sent(phase, 0)
        sent(phase, 1)
    bias_pair.wait_send()
    pltpu.make_async_copy(bias_recv.at[far], bias_recv.at[far], send_sems.at[14]).wait()
    one.left()
    two.left()
    for copy in leave:
        copy.wait()


def finish(
    in_embedding,
    in_one,
    in_two,
    in_bias,
    out_embedding,
    out_self_first,
    out_neighbour_first,
    out_bias_first,
    out_self_second,
    out_neighbour_second,
    out_bias_second,
    embedding,
    one,
    two,
    bias,
    self_first,
    neighbour_first,
    self_second,
    neighbour_second,
    sems,
):
    loads = [
        pltpu.make_async_copy(src, dst, sems.at[7 + n])
        for n, (src, dst) in enumerate(
            ((in_one, one), (in_two, two), (in_embedding, embedding), (in_bias, bias))
        )
    ]
    for load in loads:
        load.start()
    width = embedding.shape[1]
    half = width // 2
    copies = []

    def leave(src, dst):
        copies.append(pltpu.make_async_copy(src, dst, sems.at[len(copies)]))
        copies[-1].start()

    loads[0].wait()
    self_first[...] = one[0].astype(F32)
    leave(self_first, out_self_first)
    loads[1].wait()
    neighbour_first[:, :half] = two[0].astype(F32)
    neighbour_first[:, half:] = two[1].astype(F32)
    leave(neighbour_first, out_neighbour_first)
    loads[2].wait()
    leave(embedding, out_embedding)
    self_second[...] = one[1, :width].astype(F32)
    leave(self_second, out_self_second)
    neighbour_second[...] = one[1, width:].astype(F32)
    leave(neighbour_second, out_neighbour_second)
    loads[3].wait()
    leave(bias.at[:, :width], out_bias_second)
    leave(bias.at[:, width:], out_bias_first)
    for copy in copies:
        copy.wait()


def per_device(
    features,
    self_first,
    neighbour_first,
    bias_first,
    self_second,
    neighbour_second,
    bias_second,
    request_first,
    adjacent_first,
    request_second,
    adjacent_second,
    request_edges,
    edge_source,
    edge_target,
):
    nodes, feats = features.shape
    width = self_first.shape[1]
    _, peers, cap = request_first.shape
    slots = peers * cap
    edges = edge_source.shape[0]
    arguments = (
        features,
        self_first,
        neighbour_first,
        bias_first.reshape(1, width),
        self_second,
        neighbour_second,
        bias_second.reshape(1, width),
        request_first[0].T,
        adjacent_first.T,
        request_second[0].T,
        adjacent_second.T,
        request_edges[0].T,
        edge_source.reshape(1, edges),
        edge_target.reshape(1, edges),
    )
    vmem = pltpu.VMEM
    scratch = [vmem(a.shape, a.dtype) for a in arguments] + [
        vmem((nodes, width), BF),
        vmem((1, 2 * width), F32),
        pltpu.SemaphoreType.DMA((4,)),
        pltpu.SemaphoreType.DMA((14,)),
        vmem((peers, 1, 128), jnp.int32),
        vmem((peers, 1, 128), jnp.int32),
        vmem((peers, 128), jnp.int32),
        vmem((nodes, slots), BF),
        vmem((slots, nodes), BF),
        vmem((nodes, slots), BF),
        vmem((slots, nodes), BF),
        vmem((slots, nodes), BF),
        vmem((nodes, slots), BF),
        vmem((slots, nodes), BF),
        vmem((nodes, slots), BF),
        vmem((slots, nodes), BF),
        vmem((nodes, slots), BF),
        vmem((nodes, edges), BF),
        vmem((edges, nodes), BF),
        vmem((slots, edges), BF),
        vmem((edges, slots), BF),
        vmem((feats, nodes), BF),
        vmem((width, nodes), BF),
        vmem((nodes, width), F32),
        vmem((nodes, width), F32),
        vmem((nodes, width), F32),
        vmem((nodes, width), F32),
        vmem((nodes, width), BF),
        vmem((nodes, width), BF),
        vmem((nodes, width), F32),
        vmem((nodes, width), F32),
        vmem((nodes, width), F32),
        vmem((6, 2, slots, width // 2), BF),
        vmem((6, 2, slots, width // 2), BF),
        vmem((nodes, width), BF),
        vmem((nodes, width), BF),
        vmem((1, 1, 2 * width), F32),
        vmem((1, 1, 2 * width), F32),
        vmem((1, 1, 2 * width), F32),
        vmem((peers // 2, 1, 2 * width), F32),
        vmem((2, feats, width), F32),
        vmem((2, feats, width), TRAVEL),
        vmem((2, feats, width), TRAVEL),
        vmem((2, feats, width), TRAVEL),
        vmem((2, feats, width // 2), F32),
        vmem((2, feats, width // 2), TRAVEL),
        vmem((2, feats, width // 2), TRAVEL),
        vmem((2, feats, width // 2), TRAVEL),
        pltpu.SemaphoreType.DMA((24,)),
        pltpu.SemaphoreType.DMA((24,)),
    ]
    summed = pl.pallas_call(
        functools.partial(kernel, peers),
        out_shape=(
            jax.ShapeDtypeStruct((nodes, width), BF),
            jax.ShapeDtypeStruct((2, feats, width), TRAVEL),
            jax.ShapeDtypeStruct((2, feats, width // 2), TRAVEL),
            jax.ShapeDtypeStruct((1, 2 * width), F32),
        ),
        in_specs=[pl.BlockSpec(memory_space=pltpu.HBM)] * 14,
        out_specs=[pl.BlockSpec(memory_space=pltpu.HBM)] * 4,
        scratch_shapes=scratch,
        compiler_params=pltpu.CompilerParams(
            collective_id=0, has_side_effects=True, vmem_limit_bytes=60 * 2**20
        ),
    )(*arguments)
    results = pl.pallas_call(
        finish,
        out_shape=(
            jax.ShapeDtypeStruct((nodes, width), BF),
            jax.ShapeDtypeStruct((feats, width), F32),
            jax.ShapeDtypeStruct((feats, width), F32),
            jax.ShapeDtypeStruct((1, width), F32),
            jax.ShapeDtypeStruct((width, width), F32),
            jax.ShapeDtypeStruct((width, width), F32),
            jax.ShapeDtypeStruct((1, width), F32),
        ),
        in_specs=[pl.BlockSpec(memory_space=pltpu.HBM)] * 4,
        out_specs=[pl.BlockSpec(memory_space=pltpu.HBM)] * 7,
        scratch_shapes=[
            vmem((nodes, width), BF),
            vmem((2, feats, width), TRAVEL),
            vmem((2, feats, width // 2), TRAVEL),
            vmem((1, 2 * width), F32),
            vmem((feats, width), F32),
            vmem((feats, width), F32),
            vmem((width, width), F32),
            vmem((width, width), F32),
            pltpu.SemaphoreType.DMA((11,)),
        ],
        compiler_params=pltpu.CompilerParams(vmem_limit_bytes=60 * 2**20),
    )(*summed)
    return (
        results[0],
        results[1],
        results[2],
        results[3].reshape(width),
        results[4],
        results[5],
        results[6].reshape(width),
    )


def solution(mesh):
    in_specs = (
        P(("dp", "coop"), None),
        P(),
        P(),
        P(),
        P(),
        P(),
        P(),
        P(("dp", "coop"), None, None),
        P(("dp", "coop"), None),
        P(("dp", "coop"), None, None),
        P(("dp", "coop"), None),
        P(("dp", "coop"), None, None),
        P(("dp", "coop")),
        P(("dp", "coop")),
    )
    out_specs = (
        P(("dp", "coop"), None),
        P("dp", None),
        P("dp", None),
        P("dp"),
        P("dp", None),
        P("dp", None),
        P("dp"),
    )
    return jax.shard_map(
        per_device, mesh=mesh, in_specs=in_specs, out_specs=out_specs, check_vma=False
    )
```

time: 142 us -> 126 us (0.89)
  Pallas kernels: 141 us -> 126 us
    pallas_call x1, Pallas kernels: 138 us -> 123 us  [per_device(): pl.pallas_call(functools.partial(kernel, peers), out_shape=(jax.ShapeDtyp...]
where the time goes in v3:
time: 126 us
  Pallas kernels  126 us (100%)
    pallas_call x1, Pallas kernels, per_device(): pl.pallas_call(functools.partial(kernel, peers), out_shape=(jax.ShapeDtyp...  123 us

profile of v3, /device:TPU:1, one launch (start us, length us, event | category | flops | bytes accessed | tf_op | source)
XLA Modules:
  0.0 126.2 jit_solution(2177471160112973692)
XLA Ops:
  0.6 123.2 %shard_map.189 = (bf16[512,256]{1,0:T(8,128)(2,1)}, bf16[2,512,256]{2,1,0:T(8,128)(2,1)}, bf16[2,512,128]{2,1,0:T(8,128)(2,1)}, f32[1,512]{1,0:T(1,128)}) custom-call(bf16[512,512]{1,0:T(8,128)(2,1)} %refs_0_.1, bf16[512,256]{1,0:T(8,128)(2,1)} %refs_1_.1, bf16[512,256]{1,0:T(8,128)(2,1)} %refs_2_.1, f32[1,256]{1,0:T(1,128)} %bitcast.24, ...), custom_call_target="tpu_custom_call" | custom-call | tf_op jit(solution)/shard_map/pallas_call | solution.py:798
  123.8 2.4 %shard_map.190 = (bf16[512,256]{1,0:T(8,128)(2,1)}, f32[512,256]{1,0:T(8,128)}, f32[512,256]{1,0:T(8,128)}, f32[1,256]{1,0:T(1,128)}, f32[256,256]{1,0:T(8,128)}, /*index=5*/f32[256,256]{1,0:T(8,128)}, f32[1,256]{1,0:T(1,128)}) custom-call(bf16[512,256]{1,0:T(8,128)(2,1)} %get-tuple-element.18.in_embedding, bf16[2,512,256]{2,1,0:T(8,128)(2,1)} %get-tuple-element.19.in_one, ...), custom_call_target="tpu_custom_call" | custom-call | tf_op jit(solution)/shard_map/pallas_call | solution.py:813

commit v4 on v3

--- a/solution.py
+++ b/solution.py
@@ -87,7 +87,6 @@
     a1t,
     a2,
     a2t,
-    p1,
     p1t,
     p2,
     p2t,
@@ -107,6 +106,7 @@
     left,
     grad,
     own,
+    coefs,
     totals,
     sends,
     recvs,
@@ -120,12 +120,16 @@
     pair_one,
     shards_one,
     final_one,
+    lines,
     grads_two,
     pair_two,
     shards_two,
     final_two,
     send_sems,
     recv_sems,
+    group_sems,
+    partial,
+    pieces,
 ):
     me = lax.axis_index("coop")
     chip = me // 2
@@ -270,13 +274,14 @@
         lane = lax.broadcasted_iota(jnp.int32, spread.shape, 1) % 128
         return jnp.where(lane == n * cap + row % cap, spread, 0.0).astype(BF)
 
+    def picks_of(n, start):
+        part = mine(n, start)
+        wanted = nt(part, jnp.ones((nodes, part.shape[1]), BF))
+        return one_if(wanted == lax.broadcasted_iota(jnp.int32, wanted.shape, 1).astype(F32))
+
     def picks(n, matrix):
         def one(rows, start):
-            part = mine(n, start)
-            wanted = nt(part, jnp.ones((nodes, part.shape[1]), BF))
-            matrix[rows, :] = one_if(
-                wanted == lax.broadcasted_iota(jnp.int32, wanted.shape, 1).astype(F32)
-            )
+            matrix[rows, :] = picks_of(n, start)
 
         blocks(slots, step, one)
 
@@ -290,12 +295,12 @@
 
         blocks(slots, step, one)
 
-    def block(phase, side, peer):
+    def block(phase, side, peer, dx):
         return pltpu.make_async_remote_copy(
             sends.at[phase, side, pl.ds(pl.multiple_of(peer * cap, cap), cap)],
             recvs.at[phase, side, pl.ds(pl.multiple_of(me * cap, cap), cap)],
             send_sems.at[2 * phase + side],
-            recv_sems.at[2 * phase + side],
+            group_sems.at[XS * (2 * phase + side) + dx],
             device_id={"coop": peer},
             device_id_type=MESH,
         )
@@ -311,11 +316,11 @@
 
             def send(j, carry):
                 to = x * group + (chip + far_z(j)) % ZS * 2
-                block(phase, side, to + 1 - core).start()
+                block(phase, side, to + 1 - core, far_x(i)).start()
 
                 @pl.when(to + core != me)
                 def _():
-                    block(phase, side, to + core).start()
+                    block(phase, side, to + core, far_x(i)).start()
 
                 return carry
 
@@ -330,9 +335,27 @@
         most = sends.at[phase, side, pl.ds(0, (peers - 1) * cap)]
         pltpu.make_async_copy(most, most, send_sems.at[2 * phase + side]).wait()
 
-    def arrived(phase, side):
-        most = recvs.at[phase, side, pl.ds(0, (peers - 1) * cap)]
-        pltpu.make_async_copy(most, most, recv_sems.at[2 * phase + side]).wait()
+    def collect(phase, side, matrix, body):
+        for n in range(XS):
+            dx = (2, 3, 1, 0)[n]
+            count = (group if dx else group - 1) * cap
+            some = recvs.at[phase, side, pl.ds(0, count)]
+            pltpu.make_async_copy(
+                some, some, group_sems.at[XS * (2 * phase + side) + dx]
+            ).wait()
+            start = (chip // ZS + XS - dx) % XS * step
+            slots_there = pl.ds(pl.multiple_of(start, step), step)
+
+            def one(rows, start):
+                value = nn(matrix[rows, slots_there], recvs[phase, side, slots_there, :])
+                if n:
+                    value = value + partial[rows, :]
+                if n < XS - 1:
+                    partial[rows, :] = value
+                else:
+                    body(rows, start, value)
+
+            blocks(matrix.shape[0], CHUNK, one)
 
     half = width // 2
     sides = (slice(0, half), slice(half, width))
@@ -366,22 +389,23 @@
 
         ship(phase, side, one)
 
-    picks(0, p1)
-    fill(0, p1, left)
-
+    def gather_first(rows, start):
+        part = nn(picks_of(0, start), left[...]).astype(BF)
+        for side in range(2):
+            sends[0, side, rows, :] = part[:, sides[side]]
+
+    ship(0, 0, gather_first)
+    ship(0, 1, None)
     transpose(a1t, a1)
     inverse(a1, inv1)
     picks(1, p2)
     count(adjacent_second, a2t)
-    transpose(a2t, a2)
-    inverse(a2, inv2)
     picks(2, p3)
     for side in range(2):
-        arrived(0, side)
         cols = sides[side]
 
-        def layer_one(rows, start):
-            value = base[rows, cols] + nn(a1[rows, :], recvs[0, side]) * inv1[rows, cols]
+        def layer_one(rows, start, total):
+            value = base[rows, cols] + total * inv1[rows, cols]
             before[rows, cols] = value
             part = jnp.maximum(value, 0.0).astype(BF)
             hidden[rows, cols] = part
@@ -391,7 +415,7 @@
             else:
                 left[rows, :] = (totals[rows, :] + more).astype(BF)
 
-        blocks(nodes, CHUNK, layer_one)
+        collect(0, side, a1, layer_one)
 
     fill(1, p2, left)
 
@@ -399,6 +423,8 @@
         base[rows, :] = nn(hidden[rows, :], self_second[...]) + bias_second[...]
 
     blocks(nodes, CHUNK, second_base)
+    transpose(a2t, a2)
+    inverse(a2, inv2)
     vertex = lax.broadcasted_iota(jnp.int32, (nodes, edges), 0)
     source_t[...] = one_if(vertex == edge_source[...])
     slot = lax.broadcasted_iota(jnp.int32, (slots, edges), 0)
@@ -407,15 +433,12 @@
     transpose(target_t, target)
     transpose(hidden, hidden_t)
     for side in range(2):
-        arrived(1, side)
         cols = sides[side]
 
-        def layer_two(rows, start):
-            embedding[rows, cols] = (
-                base[rows, cols] + nn(a2[rows, :], recvs[1, side]) * inv2[rows, cols]
-            ).astype(BF)
-
-        blocks(nodes, CHUNK, layer_two)
+        def layer_two(rows, start, total):
+            embedding[rows, cols] = (base[rows, cols] + total * inv2[rows, cols]).astype(BF)
+
+        collect(1, side, a2, layer_two)
         fill_side(2, side, p3, embedding[:, cols])
     leave = [
         pltpu.make_async_copy(embedding, out_embedding, out_sems.at[0]),
@@ -432,18 +455,14 @@
     picks_t(2, p3t)
     transpose(features, features_t)
     picks_t(1, p2t)
-    arrived(2, 0)
-
-    def first_scores(rows, start):
-        right = nn(target[rows, :], recvs[2, 0])
+
+    def first_scores(rows, start, right):
         own[rows, sides[0]] = right
         grad[rows, sides[0]] = left[rows, sides[0]].astype(F32) * right
 
-    blocks(edges, CHUNK, first_scores)
-    arrived(2, 1)
-
-    def scores(rows, start):
-        right = nn(target[rows, :], recvs[2, 1])
+    collect(2, 0, target, first_scores)
+
+    def scores(rows, start, right):
         here = left[rows, :].astype(F32)
         products = grad[rows, sides[0]] + here[:, sides[1]] * right
         score = jnp.sum(products, axis=1, keepdims=True) * width ** (-0.5)
@@ -451,37 +470,34 @@
         label = jnp.where(edge < edges // 2, 1.0, 0.0)
         coef = (jax.nn.sigmoid(score) - label) * (edges * peers * width) ** (-0.5)
         grad[rows, :] = coef * here
-        own[rows, sides[0]] = coef * own[rows, sides[0]]
-        own[rows, sides[1]] = coef * right
-
-    blocks(edges, CHUNK, scores)
+        own[rows, sides[1]] = right
+        coefs[rows, :] = coef
+
+    collect(2, 1, target, scores)
     for side in range(2):
         fill_split(3, side, target_t, grad[:, sides[side]])
-    high, low = split(own[...])
+    high, low = split(coefs[...] * own[...])
     totals[...] = nn(source_t[...], high) + nn(source_t[...], low)
     picks_t(0, p1t)
     for side in range(2):
-        arrived(3, side)
         cols = sides[side]
 
-        def outer(rows, start):
-            grad[rows, cols] = totals[rows, cols] + nn(p3t[rows, :], recvs[3, side])
-
-        blocks(nodes, CHUNK, outer)
+        def outer(rows, start, total):
+            grad[rows, cols] = totals[rows, cols] + total
+
+        collect(3, side, p3t, outer)
         fill_split(4, side, a2t, grad[:, cols] * inv2[:, cols])
     bias_send[:, :, :width] = jnp.sum(grad[...], axis=0, keepdims=True)[None]
     outer_round = grad[...].astype(BF)
     grads_one[1, :width, :] = nn(hidden_t[...], outer_round)
     own[...] = nt(outer_round, self_second[...])
     for side in range(2):
-        arrived(4, side)
         cols = sides[side]
         weight = neighbour_second[:, cols]
         weights = jnp.concatenate([weight, weight], axis=1)
 
-        def second_totals(rows, start):
-            value = nn(p2t[rows, :], recvs[4, side])
-            high, low = split(value)
+        def second_totals(rows, start, total):
+            high, low = split(total)
             highs[rows, cols] = high
             lows[rows, cols] = low
             value = own[rows, :] + nt(jnp.concatenate([high, low], axis=1), weights)
@@ -490,11 +506,9 @@
             else:
                 grad[rows, :] = jnp.where(before[rows, :] > 0.0, value, 0.0)
 
-        blocks(nodes, CHUNK, second_totals)
-
-    for side in range(2):
-        cols = sides[side]
-        fill_split(5, side, a1t, grad[:, cols] * inv1[:, cols])
+        collect(4, side, p2t, second_totals)
+
+    fill_split(5, 0, a1t, grad[:, sides[0]] * inv1[:, sides[0]])
     inner_round = grad[...].astype(BF)
 
     def self_gradient(rows, start):
@@ -507,119 +521,144 @@
     place = pl.ds(pl.multiple_of(chip * share, share), share)
     partner = chip * 2 + 1 - core
 
-    class Summing:
-        def __init__(self, grads, pair, shards, final, first_sem):
-            self.grads, self.pair, self.shards, self.final = grads, pair, shards, final
-            self.sem = first_sem
-            self.swap = self.to_partner(pair.at[0], pair.at[1], 0)
-            self.back = self.to_partner(final.at[core], final.at[core], 3)
-
-        def to_partner(self, src, dst, n):
-            return pltpu.make_async_remote_copy(
-                src,
-                dst,
-                send_sems.at[self.sem + n],
-                recv_sems.at[self.sem + n],
-                device_id={"coop": partner},
-                device_id_type=MESH,
-            )
-
-        def to_chips(self, src_of, dst, n):
-            def send(to):
-                pltpu.make_async_remote_copy(
-                    src_of(to),
-                    dst,
-                    send_sems.at[self.sem + n],
-                    recv_sems.at[self.sem + n],
-                    device_id={"coop": to * 2 + core},
-                    device_id_type=MESH,
-                ).start()
-
-            to_others(send)
-
-        def all_of(self, sem):
-            most = self.shards.at[1, pl.ds(0, (chips - 1) * share)]
-            pltpu.make_async_copy(most, most, sem).wait()
-
-        def start(self):
-            self.pair[0] = self.grads[1 - core].astype(TRAVEL)
-            self.swap.start()
-
-        def add_pair(self):
-            self.swap.wait_recv()
-            self.shards[0] = (self.grads[core] + self.pair[1].astype(F32)).astype(TRAVEL)
-
-        def scatter(self):
-            self.to_chips(
-                lambda to: self.shards.at[0, pl.ds(pl.multiple_of(to * share, share), share)],
-                self.shards.at[1, place],
-                1,
-            )
-            self.shards[1, place, :] = self.shards[0, place, :]
-
-        def gather(self):
-            self.all_of(recv_sems.at[self.sem + 1])
-            total = self.shards[1, 0:share, :].astype(F32)
-            for c in range(1, chips):
-                total = total + self.shards[1, c * share : (c + 1) * share, :].astype(F32)
-            self.final[core, place, :] = total.astype(TRAVEL)
-            mine = self.final.at[core, place]
-            self.to_chips(lambda to: mine, mine, 2)
-
-        def give_back(self):
-            self.all_of(recv_sems.at[self.sem + 2])
-            self.back.start()
-
-        def left(self):
-            self.swap.wait_send()
-            self.all_of(send_sems.at[self.sem + 1])
-            self.all_of(send_sems.at[self.sem + 2])
-            self.back.wait_send()
-
-    one = Summing(grads_one, pair_one, shards_one, final_one, 16)
-    two = Summing(grads_two, pair_two, shards_two, final_two, 20)
-    one.start()
-    bias_send[:, :, width:] = jnp.sum(grad[...], axis=0, keepdims=True)[None]
-    bias_pair = pltpu.make_async_remote_copy(
-        bias_send,
-        bias_near,
-        send_sems.at[13],
-        recv_sems.at[13],
-        device_id={"coop": partner},
-        device_id_type=MESH,
-    )
-    bias_pair.start()
-    one.add_pair()
-    bias_pair.wait_recv()
-    bias_held[...] = bias_send[...] + bias_near[...]
-    sent(5, 0)
-    sent(5, 1)
-    one.scatter()
-
-    def spread_bias(to):
+    def to_partner(src, dst, sem):
+        return pltpu.make_async_remote_copy(
+            src,
+            dst,
+            send_sems.at[sem],
+            recv_sems.at[sem],
+            device_id={"coop": partner},
+            device_id_type=MESH,
+        )
+
+    def send_rows(src, dst, sem, to):
         pltpu.make_async_remote_copy(
-            bias_held.at[0],
-            bias_recv.at[chip],
-            send_sems.at[14],
-            recv_sems.at[14],
+            src,
+            dst,
+            send_sems.at[sem],
+            recv_sems.at[sem],
             device_id={"coop": to * 2 + core},
             device_id_type=MESH,
         ).start()
 
-    to_others(spread_bias)
+    def to_x(start):
+        for dx in (2, 1, 3):
+            start((chip // ZS + dx) % XS)
+
+    def to_z(start):
+        for dz in (4, 3, 5, 2, 6, 1, 7):
+            start((chip % ZS + dz) % ZS)
+
+    def await_rows(ref, count, sem):
+        rows = ref.at[pl.ds(0, count)]
+        pltpu.make_async_copy(rows, rows, sem).wait()
+
+    my_x, my_z = chip // ZS, chip % ZS
+    tall = ZS * share
+    x_rows = lambda x: pl.ds(pl.multiple_of(x * tall, tall), tall)
+    z_rows = lambda z: pl.ds(pl.multiple_of(z * share, share), share)
+
+    def summed(ref, count, rows):
+        total = ref[0:rows, :].astype(F32)
+        for c in range(1, count):
+            total = total + ref[c * rows : (c + 1) * rows, :].astype(F32)
+        return total
+
+    one_swap = to_partner(pair_one.at[0], pair_one.at[1], 16)
+    one_back = to_partner(final_one.at[core], final_one.at[core], 17)
+    x_send, x_recv = shards_one.at[0], shards_one.at[1]
+    z_send, z_recv = lines.at[0], lines.at[1]
+    final_mine = final_one.at[core]
+
+    def one_along_x():
+        one_swap.wait_recv()
+        x_send[...] = (grads_one[core] + pair_one[1].astype(F32)).astype(TRAVEL)
+        to_x(lambda x: send_rows(x_send.at[x_rows(x)], x_recv.at[x_rows(my_x)], 18, x * ZS + my_z))
+        x_recv[x_rows(my_x), :] = x_send[x_rows(my_x), :]
+
+    def one_along_z():
+        await_rows(x_recv, (XS - 1) * tall, recv_sems.at[18])
+        z_send[...] = summed(x_recv, XS, tall).astype(TRAVEL)
+        to_z(lambda z: send_rows(z_send.at[z_rows(z)], z_recv.at[z_rows(my_z)], 19, my_x * ZS + z))
+        z_recv[z_rows(my_z), :] = z_send[z_rows(my_z), :]
+
+    def one_gather_z():
+        await_rows(z_recv, (ZS - 1) * share, recv_sems.at[19])
+        final_one[core, place, :] = summed(z_recv, ZS, share).astype(TRAVEL)
+        here = final_mine.at[place]
+        to_z(lambda z: send_rows(here, here, 20, my_x * ZS + z))
+
+    def one_gather_x():
+        await_rows(z_recv, (ZS - 1) * share, recv_sems.at[20])
+        here = final_mine.at[x_rows(my_x)]
+        to_x(lambda x: send_rows(here, here, 21, x * ZS + my_z))
+
+    def one_give_back():
+        await_rows(x_recv, (XS - 1) * tall, recv_sems.at[21])
+        one_back.start()
+
+    two_swap = to_partner(pair_two.at[0], pair_two.at[1], 22)
+    two_back = to_partner(final_two.at[core], final_two.at[core], 23)
+    two_send, two_recv = shards_two.at[0], shards_two.at[1]
+
+    def two_swap_side(side):
+        @pl.when(core != side)
+        def _():
+            pair_two[0] = grads_two[side].astype(TRAVEL)
+            two_swap.start()
+
+        @pl.when(core == side)
+        def _():
+            two_swap.wait_recv()
+            two_send[...] = (grads_two[side] + pair_two[1].astype(F32)).astype(TRAVEL)
+            to_others(
+                lambda to: send_rows(
+                    two_send.at[pl.ds(pl.multiple_of(to * share, share), share)],
+                    two_recv.at[place],
+                    12,
+                    to,
+                )
+            )
+            two_recv[place, :] = two_send[place, :]
+
+    def two_gather():
+        await_rows(two_recv, (chips - 1) * share, recv_sems.at[12])
+        final_two[core, place, :] = summed(two_recv, chips, share).astype(TRAVEL)
+        here = final_two.at[core, place]
+        to_others(lambda to: send_rows(here, here, 24, to))
+
+    def two_give_back():
+        await_rows(two_recv, (chips - 1) * share, recv_sems.at[24])
+        two_back.start()
+
+    pair_one[0] = grads_one[1 - core].astype(TRAVEL)
+    one_swap.start()
+    bias_send[:, :, width:] = jnp.sum(grad[...], axis=0, keepdims=True)[None]
+    bias_pair = to_partner(bias_send, bias_near, 13)
+    bias_pair.start()
+    one_along_x()
+    fill_split(5, 1, a1t, grad[:, sides[1]] * inv1[:, sides[1]])
+    bias_pair.wait_recv()
+    bias_held[...] = bias_send[...] + bias_near[...]
+    to_others(lambda to: send_rows(bias_held.at[0], bias_recv.at[chip], 14, to))
     bias_recv[pl.ds(chip, 1)] = bias_held[...]
-    for side in range(2):
-        arrived(5, side)
-        pieces = joined(nn(p1t[...], recvs[5, side]))
+
+    def near(side):
+        def first_totals(rows, start, total):
+            pieces[rows, :] = joined(total)
+
+        collect(5, side, p1t, first_totals)
 
         def near_gradient(rows, start):
-            grads_two[side, rows, :] = folded(nn(features_t[rows, :], pieces))
+            grads_two[side, rows, :] = folded(nn(features_t[rows, :], pieces[...]))
 
         blocks(feats, CHUNK, near_gradient)
-    two.start()
-    two.add_pair()
-    two.scatter()
-    one.gather()
+        two_swap_side(side)
+
+    near(0)
+    one_along_z()
+    near(1)
+    one_gather_z()
     far = pl.ds(0, chips - 1)
     pltpu.make_async_copy(bias_recv.at[far], bias_recv.at[far], recv_sems.at[14]).wait()
     total = bias_recv[0]
@@ -627,22 +666,31 @@
         total = total + bias_recv[c]
     bias_total[...] = total
     leave[1].start()
-    two.gather()
-    one.give_back()
-    two.give_back()
-    one.back.wait_recv()
+    one_gather_x()
+    two_gather()
+    one_give_back()
+    two_give_back()
+    one_back.wait_recv()
     leave[2].start()
-    two.back.wait_recv()
+    two_back.wait_recv()
     leave[3].start()
 
     pltpu.make_async_copy(ask_send.at[others], ask_send.at[others], send_sems.at[15]).wait()
-    for phase in range(5):
+    for phase in range(6):
         sent(phase, 0)
         sent(phase, 1)
     bias_pair.wait_send()
     pltpu.make_async_copy(bias_recv.at[far], bias_recv.at[far], send_sems.at[14]).wait()
-    one.left()
-    two.left()
+    one_swap.wait_send()
+    await_rows(x_recv, (XS - 1) * tall, send_sems.at[18])
+    await_rows(z_recv, (ZS - 1) * share, send_sems.at[19])
+    await_rows(z_recv, (ZS - 1) * share, send_sems.at[20])
+    await_rows(x_recv, (XS - 1) * tall, send_sems.at[21])
+    one_back.wait_send()
+    two_swap.wait_send()
+    await_rows(two_recv, (chips - 1) * share, send_sems.at[12])
+    await_rows(two_recv, (chips - 1) * share, send_sems.at[24])
+    two_back.wait_send()
     for copy in leave:
         copy.wait()
 
@@ -755,7 +803,6 @@
         vmem((slots, nodes), BF),
         vmem((nodes, slots), BF),
         vmem((slots, nodes), BF),
-        vmem((slots, nodes), BF),
         vmem((nodes, slots), BF),
         vmem((slots, nodes), BF),
         vmem((nodes, slots), BF),
@@ -775,6 +822,7 @@
         vmem((nodes, width), BF),
         vmem((nodes, width), F32),
         vmem((nodes, width), F32),
+        vmem((edges, 1), F32),
         vmem((nodes, width), F32),
         vmem((6, 2, slots, width // 2), BF),
         vmem((6, 2, slots, width // 2), BF),
@@ -788,12 +836,16 @@
         vmem((2, feats, width), TRAVEL),
         vmem((2, feats, width), TRAVEL),
         vmem((2, feats, width), TRAVEL),
+        vmem((2, feats // XS, width), TRAVEL),
         vmem((2, feats, width // 2), F32),
         vmem((2, feats, width // 2), TRAVEL),
         vmem((2, feats, width // 2), TRAVEL),
         vmem((2, feats, width // 2), TRAVEL),
-        pltpu.SemaphoreType.DMA((24,)),
-        pltpu.SemaphoreType.DMA((24,)),
+        pltpu.SemaphoreType.DMA((25,)),
+        pltpu.SemaphoreType.DMA((25,)),
+        pltpu.SemaphoreType.DMA((12 * XS,)),
+        vmem((nodes, width // 2), F32),
+        vmem((nodes, width), BF),
     ]
     summed = pl.pallas_call(
         functools.partial(kernel, peers),

time: 126 us -> 122 us (0.968)
  Pallas kernels: 126 us -> 121 us
    pallas_call x1, Pallas kernels: 123 us -> 118 us  [per_device(): pl.pallas_call(functools.partial(kernel, peers), out_shape=(jax.ShapeDtyp...]
where the time goes in v4:
time: 122 us
  Pallas kernels  121 us (99%)
    pallas_call x1, Pallas kernels, per_device(): pl.pallas_call(functools.partial(kernel, peers), out_shape=(jax.ShapeDtyp...  118 us

profile of v4, /device:TPU:1, one launch (start us, length us, event | category | flops | bytes accessed | tf_op | source)
XLA Modules:
  0.0 121.5 jit_solution(7562489515230939215)
XLA Ops:
  0.6 118.5 %shard_map.189 = (bf16[512,256]{1,0:T(8,128)(2,1)}, bf16[2,512,256]{2,1,0:T(8,128)(2,1)}, bf16[2,512,128]{2,1,0:T(8,128)(2,1)}, f32[1,512]{1,0:T(1,128)}) custom-call(bf16[512,512]{1,0:T(8,128)(2,1)} %refs_0_.1, bf16[512,256]{1,0:T(8,128)(2,1)} %refs_1_.1, bf16[512,256]{1,0:T(8,128)(2,1)} %refs_2_.1, f32[1,256]{1,0:T(1,128)} %bitcast.24, ...), custom_call_target="tpu_custom_call" | custom-call | tf_op jit(solution)/shard_map/pallas_call | solution.py:850
  119.1 2.4 %shard_map.190 = (bf16[512,256]{1,0:T(8,128)(2,1)}, f32[512,256]{1,0:T(8,128)}, f32[512,256]{1,0:T(8,128)}, f32[1,256]{1,0:T(1,128)}, f32[256,256]{1,0:T(8,128)}, /*index=5*/f32[256,256]{1,0:T(8,128)}, f32[1,256]{1,0:T(1,128)}) custom-call(bf16[512,256]{1,0:T(8,128)(2,1)} %get-tuple-element.18.in_embedding, bf16[2,512,256]{2,1,0:T(8,128)(2,1)} %get-tuple-element.19.in_one, ...), custom_call_target="tpu_custom_call" | custom-call | tf_op jit(solution)/shard_map/pallas_call | solution.py:865

commit v5 on v4

--- a/solution.py
+++ b/solution.py
@@ -30,7 +30,7 @@
         body(far_x(n // ZS), far_z(n % ZS))
         return carry
 
-    lax.fori_loop(0, XS * ZS, one, 0)
+    lax.fori_loop(0, XS * ZS, one, 0, unroll=ZS)
 
 
 def nn(a, b):
@@ -143,11 +143,11 @@
     def to_all(start):
         def both(x, z):
             to = chip_at(x, z) * 2
-            start(to + 1 - core)
+            start(to + 1 - core, x)
 
             @pl.when(to + core != me)
             def _():
-                start(to + core)
+                start(to + core, x)
 
         every(both)
 
@@ -161,7 +161,7 @@
 
         every(one)
 
-    def greet(peer):
+    def greet(peer, x):
         pl.semaphore_signal(barrier, inc=1, device_id={"coop": peer}, device_id_type=MESH)
 
     to_all(greet)
@@ -239,12 +239,12 @@
 
     pl.semaphore_wait(barrier, peers - 1)
 
-    def ask(peer):
+    def ask(peer, x):
         pltpu.make_async_remote_copy(
             ask_send.at[peer],
             ask_recv.at[me],
             send_sems.at[15],
-            recv_sems.at[15],
+            group_sems.at[12 * XS + x],
             device_id={"coop": peer},
             device_id_type=MESH,
         ).start()
@@ -259,18 +259,24 @@
     count(adjacent_first, a1t)
 
     others = pl.ds(0, peers - 1)
-    pltpu.make_async_copy(ask_recv.at[others], ask_recv.at[others], recv_sems.at[15]).wait()
-    for d in range(peers):
-        asked[d : d + 1, :] = ask_recv[d]
+    group = 2 * ZS
+
+    def asks_from(i):
+        dx = (XS - (2, 3, 1, 0)[i]) % XS
+        some = ask_recv.at[pl.ds(0, group if dx else group - 1)]
+        pltpu.make_async_copy(some, some, group_sems.at[12 * XS + dx]).wait()
+        first = (chip // ZS + XS - dx) % XS * group
+        for d in range(group):
+            asked[pl.ds(first + d, 1), :] = ask_recv[first + d]
 
     def mine(n, start):
-        table = asked[...]
+        table = asked[pl.ds(pl.multiple_of(start // cap, group), group), :]
         low = table % 16
         parts = jnp.concatenate([table - low, low], axis=1).astype(F32).astype(BF)
-        row = lax.broadcasted_iota(jnp.int32, (step, peers), 0) + start
-        owner = lax.broadcasted_iota(jnp.int32, (step, peers), 1)
+        row = lax.broadcasted_iota(jnp.int32, (step, group), 0)
+        owner = lax.broadcasted_iota(jnp.int32, (step, group), 1)
         spread = nn(one_if(row // cap == owner), parts)
-        row = lax.broadcasted_iota(jnp.int32, spread.shape, 0) + start
+        row = lax.broadcasted_iota(jnp.int32, spread.shape, 0)
         lane = lax.broadcasted_iota(jnp.int32, spread.shape, 1) % 128
         return jnp.where(lane == n * cap + row % cap, spread, 0.0).astype(BF)
 
@@ -305,9 +311,7 @@
             device_id_type=MESH,
         )
 
-    group = 2 * ZS
-
-    def ship(phase, side, body):
+    def ship(phase, side, body, ahead=None):
         def one(i, carry):
             x = (chip // ZS + far_x(i)) % XS
             start = x * step
@@ -324,10 +328,15 @@
 
                 return carry
 
-            lax.fori_loop(0, ZS, send, 0)
+            lax.fori_loop(0, ZS, send, 0, unroll=True)
             return carry
 
-        lax.fori_loop(0, XS, one, 0)
+        if ahead is None:
+            lax.fori_loop(0, XS, one, 0)
+        else:
+            for i in range(XS):
+                ahead(i)
+                one(i, 0)
         mine = pl.ds(pl.multiple_of(me * cap, cap), cap)
         recvs[phase, side, mine, :] = sends[phase, side, mine, :]
 
@@ -394,7 +403,7 @@
         for side in range(2):
             sends[0, side, rows, :] = part[:, sides[side]]
 
-    ship(0, 0, gather_first)
+    ship(0, 0, gather_first, asks_from)
     ship(0, 1, None)
     transpose(a1t, a1)
     inverse(a1, inv1)
@@ -843,7 +852,7 @@
         vmem((2, feats, width // 2), TRAVEL),
         pltpu.SemaphoreType.DMA((25,)),
         pltpu.SemaphoreType.DMA((25,)),
-        pltpu.SemaphoreType.DMA((12 * XS,)),
+        pltpu.SemaphoreType.DMA((13 * XS,)),
         vmem((nodes, width // 2), F32),
         vmem((nodes, width), BF),
     ]

time: 122 us -> 121 us (level)
    pallas_call x1, Pallas kernels: 118 us -> 117 us  [per_device(): pl.pallas_call(functools.partial(kernel, peers), out_shape=(jax.ShapeDtyp...]
where the time goes in v5:
time: 121 us; the launch traced here: 120 us
  Pallas kernels  120 us (99%)
    pallas_call x1, Pallas kernels, per_device(): pl.pallas_call(functools.partial(kernel, peers), out_shape=(jax.ShapeDtyp...  117 us

profile of v5, /device:TPU:1, one launch (start us, length us, event | category | flops | bytes accessed | tf_op | source)
XLA Modules:
  0.0 120.4 jit_solution(17211405739708224465)
XLA Ops:
  0.6 117.2 %shard_map.189 = (bf16[512,256]{1,0:T(8,128)(2,1)}, bf16[2,512,256]{2,1,0:T(8,128)(2,1)}, bf16[2,512,128]{2,1,0:T(8,128)(2,1)}, f32[1,512]{1,0:T(1,128)}) custom-call(bf16[512,512]{1,0:T(8,128)(2,1)} %refs_0_.1, bf16[512,256]{1,0:T(8,128)(2,1)} %refs_1_.1, bf16[512,256]{1,0:T(8,128)(2,1)} %refs_2_.1, f32[1,256]{1,0:T(1,128)} %bitcast.24, ...), custom_call_target="tpu_custom_call" | custom-call | tf_op jit(solution)/shard_map/pallas_call | solution.py:859
  117.8 2.4 %shard_map.190 = (bf16[512,256]{1,0:T(8,128)(2,1)}, f32[512,256]{1,0:T(8,128)}, f32[512,256]{1,0:T(8,128)}, f32[1,256]{1,0:T(1,128)}, f32[256,256]{1,0:T(8,128)}, /*index=5*/f32[256,256]{1,0:T(8,128)}, f32[1,256]{1,0:T(1,128)}) custom-call(bf16[512,256]{1,0:T(8,128)(2,1)} %get-tuple-element.18.in_embedding, bf16[2,512,256]{2,1,0:T(8,128)(2,1)} %get-tuple-element.19.in_one, ...), custom_call_target="tpu_custom_call" | custom-call | tf_op jit(solution)/shard_map/pallas_call | solution.py:874
